TPU v7x, 256 devices: a whole 4x4x8 slice. The times are simulated.
256 devices in a mesh: row: 16 (over y, x), col: 16 (over z, core).
Axes of the slice: x: 4, y: 4, z: 8, core: 2. Of those that a mesh axis runs over, the one named last changes fastest.
Arguments:
- embedding: bfloat16 [1024, 1024, 256], P('row', 'col'), may hold values from -6 to 6
- counts: int32 [16, 16], P('col'), may hold values from 1 to 48, 256 in all within a row
- points: int32 [16, 16, 2, 48], P('row', 'col'), may hold values from 0 to 1023
- pe_gauss: float32 [2, 128], replicated, may hold values from -6 to 6
- point_embed: float32 [256], replicated, may hold values from -6 to 6
- mask_token: float32 [256], replicated, may hold values from -6 to 6
- sa_qkv: bfloat16 [256, 768], replicated, may hold values from -0.375 to 0.375
- sa_out: bfloat16 [256, 256], replicated, may hold values from -0.375 to 0.375
- t2i_qkv: bfloat16 [256, 384], replicated, may hold values from -0.375 to 0.375
- t2i_out: bfloat16 [128, 256], replicated, may hold values from -0.5 to 0.5
- mlp_up: bfloat16 [256, 2048], replicated, may hold values from -0.375 to 0.375
- mlp_down: bfloat16 [2048, 256], replicated, may hold values from -0.125 to 0.125
- i2t_qkv: bfloat16 [256, 384], replicated, may hold values from -0.375 to 0.375
- i2t_out: bfloat16 [128, 256], replicated, may hold values from -0.5 to 0.5
- hyper_w: bfloat16 [2, 256, 256], replicated, may hold values from -0.375 to 0.375
- ln_gains: float32 [4, 256], replicated, may hold values from 0.1 to 1.9
Outputs:
- mask_logits: bfloat16 [16, 16, 48, 4096], P('row', 'col')
- seam_blend: float32 [1024, 1024], P('row', 'col')
Inputs may be any that keep to these rules, and one draw needn't show every extreme that they name: For each column index the counts of its 16 tiles sum to 256, and the largest of them is 48. `points`: slots at or past a tile's count hold coordinates that no output reads.
All inputs are finite; a program needn't handle non-finite values.
Results may differ from a plain program's by a relative error of at most 0.012.
Values may be sent and summed in bfloat16 or wider, within the bound.
A program may use at most 128 MiB of HBM per device.

v0:
```python
import math

import jax
import jax.numpy as jnp
from jax import lax
from jax.sharding import PartitionSpec as P

HEADS = 8
SEAM = 4
IMG = 1024


norm_eps = 1e-05
highest = lax.Precision.HIGHEST


def sent_to_all(value, axis):
    copies = jnp.broadcast_to(value, (lax.axis_size(axis), *value.shape))
    return lax.all_to_all(copies, axis, split_axis=0, concat_axis=0, tiled=True)


def laid_out(parts, dim):
    shape = list(parts.shape[1:])
    shape[dim] *= parts.shape[0]
    return jnp.moveaxis(parts, 0, dim).reshape(shape)


def gather_directly(value, axis, dim):
    parts = sent_to_all(value, axis)
    return laid_out(parts, dim)


def side_by_side(arrays, axis, dim, along):
    columns = [a.reshape(*a.shape[:along], -1) for a in arrays]
    both = jnp.concatenate(columns, axis=along)
    result, at, gathered = (gather_directly(both, axis, dim), 0, [])
    for a, column in zip(arrays, columns):
        slab = result[..., at : at + column.shape[along]]
        gathered.append(slab.reshape(*slab.shape[:along], *a.shape[along:]))
        at += column.shape[along]
    return tuple(gathered)


def split_up(value, dim, length):
    shape = value.shape
    parts = value.reshape(*shape[:dim], length, shape[dim] // length, *shape[dim + 1 :])
    return jnp.moveaxis(parts, dim, 0)


def cut_rows(length, count):
    step = length // count
    if step >= 8:
        step -= step % 8
    return [step * k for k in range(1, count)]


def several_exchanges(value, axis, pieces, split_dim, concat_dim):
    parts = split_up(value, split_dim, lax.axis_size(axis))
    split_at = max(range(1, max(2, parts.ndim - 1)), key=lambda d: parts.shape[d])
    gathered = []
    for slab in jnp.split(parts, cut_rows(parts.shape[split_at], pieces), axis=split_at):
        if slab.size:
            gathered.append(lax.all_to_all(slab, axis, split_axis=0, concat_axis=0, tiled=True))
    return laid_out(jnp.concatenate(gathered, axis=split_at), concat_dim)


def padded_2(cells, sides, width):
    for axis, dim in sides:
        count = lax.axis_size(axis)
        ends = count - 1
        head = lax.slice_in_dim(cells, 0, width, axis=dim)
        tail = lax.slice_in_dim(cells, cells.shape[dim] - width, cells.shape[dim], axis=dim)
        cells = jnp.concatenate(
            [
                lax.ppermute(tail, axis, [(i, (i + 1) % count) for i in range(ends)]),
                cells,
                lax.ppermute(head, axis, [((i + 1) % count, i) for i in range(ends)]),
            ],
            axis=dim,
        )
    return cells


def layer_norm(values, norm_gain):
    row_mean = jnp.mean(values, axis=-1, keepdims=True)
    centred = values - row_mean
    row_var = jnp.mean(centred * centred, axis=-1, keepdims=True)
    return centred * lax.rsqrt(row_var + norm_eps) * norm_gain


def weight_dot(values, weight):
    return jnp.dot(values, weight.astype(jnp.float32), precision=highest)


def fourier(norm_x, norm_y, pe_gauss):
    phases = (
        2.0
        * math.pi
        * (
            (2.0 * norm_x - 1.0)[:, None] * pe_gauss[0]
            + (2.0 * norm_y - 1.0)[:, None] * pe_gauss[1]
        )
    )
    return jnp.concatenate([jnp.sin(phases), jnp.cos(phases)], axis=-1)


def dense_pe(pixel_ids, grid_side, pe_gauss):
    norm_x = ((pixel_ids % grid_side).astype(jnp.float32) + 0.5) / grid_side
    norm_y = ((pixel_ids // grid_side).astype(jnp.float32) + 0.5) / grid_side
    return fourier(norm_x, norm_y, pe_gauss)


def softmax_last(scores):
    row_top = jnp.max(scores, axis=-1, keepdims=True)
    exp_scores = jnp.exp(scores - row_top)
    return exp_scores / jnp.sum(exp_scores, axis=-1, keepdims=True)


def head_select(inner_width):
    channel_head = jnp.arange(inner_width, dtype=jnp.int32) // (inner_width // HEADS)
    return jnp.arange(HEADS, dtype=jnp.int32)[:, None] == channel_head[None, :]


def token_side(
    points_xy,
    keys_pe,
    tile_flat,
    pe_gauss,
    point_embed,
    mask_token,
    sa_qkv,
    sa_out,
    t2i_qkv,
    t2i_out,
    mlp_up,
    mlp_down,
    i2t_qkv,
    hyper_w,
    ln_gains,
):
    slot_count = points_xy.shape[1]
    model_width = keys_pe.shape[1]
    inner_width = t2i_qkv.shape[1] // 3
    self_width = model_width // HEADS
    head_width = inner_width // HEADS
    coords = (points_xy.astype(jnp.float32) + 0.5) / IMG
    prompt = fourier(coords[0], coords[1], pe_gauss) + point_embed
    start_tok = jnp.stack([jnp.broadcast_to(mask_token, (slot_count, model_width)), prompt], axis=1)
    self_qkv = weight_dot(start_tok, sa_qkv).reshape(slot_count, 2, 3, HEADS, self_width)
    self_score = jnp.einsum(
        "cqhd,ckhd->chqk", self_qkv[:, :, 0], self_qkv[:, :, 1], precision=highest
    ) / math.sqrt(self_width)
    self_out = jnp.einsum(
        "chqk,ckhd->cqhd", softmax_last(self_score), self_qkv[:, :, 2], precision=highest
    )
    queries = layer_norm(
        weight_dot(self_out.reshape(slot_count, 2, model_width), sa_out), ln_gains[0]
    )
    cross_q = weight_dot(queries + start_tok, t2i_qkv[:, :inner_width]).astype(jnp.bfloat16)
    cross_k = jnp.dot(
        keys_pe, t2i_qkv[:, inner_width : 2 * inner_width], preferred_element_type=jnp.float32
    ).astype(jnp.bfloat16)
    cross_v = jnp.dot(
        tile_flat, t2i_qkv[:, 2 * inner_width :], preferred_element_type=jnp.float32
    ).astype(jnp.bfloat16)
    selector = head_select(inner_width)
    masked_q = jnp.where(
        selector[None], cross_q.reshape(slot_count * 2, 1, inner_width), jnp.zeros((), jnp.bfloat16)
    )
    masked_q = masked_q.reshape(slot_count * 2 * HEADS, inner_width)
    cross_score = lax.dot_general(
        masked_q, cross_k, (((1,), (1,)), ((), ())), preferred_element_type=jnp.float32
    ) / math.sqrt(head_width)
    cross_prob = softmax_last(cross_score).astype(jnp.bfloat16)
    head_out = jnp.dot(cross_prob, cross_v, preferred_element_type=jnp.float32).reshape(
        slot_count * 2, HEADS, inner_width
    )
    cross_out = jnp.sum(jnp.where(selector[None], head_out, 0.0), axis=1)
    queries = layer_norm(
        queries + weight_dot(cross_out.reshape(slot_count, 2, inner_width), t2i_out), ln_gains[1]
    )
    hidden = jax.nn.relu(weight_dot(queries, mlp_up))
    queries = layer_norm(queries + weight_dot(hidden, mlp_down), ln_gains[2])
    back_k = weight_dot(queries + start_tok, i2t_qkv[:, inner_width : 2 * inner_width]).astype(
        jnp.bfloat16
    )
    back_v = weight_dot(queries, i2t_qkv[:, 2 * inner_width :]).astype(jnp.bfloat16)
    kv_rows = jnp.concatenate([back_k, back_v], axis=1)
    hyper_rows = weight_dot(jax.nn.relu(weight_dot(queries[:, 0], hyper_w[0])), hyper_w[1]).astype(
        jnp.bfloat16
    )
    return (kv_rows, hyper_rows)


def image_side(tile_rows, query_rows, kv_rows, hyper_rows, out_weight, norm_gain):
    batch_rows, pix_rows, inner_width = query_rows.shape
    head_width = inner_width // HEADS
    channel_head = jnp.arange(inner_width, dtype=jnp.int32) // head_width
    same_head = (channel_head[:, None] == channel_head[None, :]).astype(jnp.float32)
    key_gap = kv_rows[:, 0].astype(jnp.float32) - kv_rows[:, 1].astype(jnp.float32)
    value_first = kv_rows[:, 2].astype(jnp.float32)
    value_second = kv_rows[:, 3].astype(jnp.float32)
    products = query_rows.astype(jnp.float32) * key_gap[:, None, :]
    score_gap = jnp.dot(
        products.reshape(batch_rows * pix_rows, inner_width), same_head, precision=highest
    )
    weight_first = jax.nn.sigmoid(score_gap / math.sqrt(head_width)).reshape(
        batch_rows, pix_rows, inner_width
    )
    mixture = value_second[:, None, :] + weight_first * (value_first - value_second)[:, None, :]
    mixture = mixture.astype(jnp.bfloat16)
    update = jnp.einsum("bpi,id->bpd", mixture, out_weight, preferred_element_type=jnp.float32)
    normed = layer_norm(tile_rows.astype(jnp.float32) + update, norm_gain)
    model_width = normed.shape[-1]
    return (
        jnp.sum(normed * hyper_rows.astype(jnp.float32)[:, None, :], axis=-1)
        / math.sqrt(model_width)
    ).astype(jnp.bfloat16)


def shards(
    embedding,
    counts,
    points,
    pe_gauss,
    point_embed,
    mask_token,
    sa_qkv,
    sa_out,
    t2i_qkv,
    t2i_out,
    mlp_up,
    mlp_down,
    i2t_qkv,
    i2t_out,
    hyper_w,
    ln_gains,
):
    grid_side = embedding.shape[0]
    model_width = embedding.shape[2]
    inner_width = t2i_qkv.shape[1] // 3
    slot_count = points.shape[3]
    pixel_count = grid_side * grid_side
    tile_flat = embedding.reshape(pixel_count, model_width)
    image_pe = dense_pe(jnp.arange(pixel_count, dtype=jnp.int32), grid_side, pe_gauss)
    keys_pe = (tile_flat.astype(jnp.float32) + image_pe).astype(jnp.bfloat16)
    kv_rows, hyper_rows = token_side(
        points[0, 0],
        keys_pe,
        tile_flat,
        pe_gauss,
        point_embed,
        mask_token,
        sa_qkv,
        sa_out,
        t2i_qkv,
        t2i_out,
        mlp_up,
        mlp_down,
        i2t_qkv,
        hyper_w,
        ln_gains,
    )
    query_weight = i2t_qkv[:, :inner_width]
    row_index = lax.axis_index("row")
    row_count = lax.axis_size("row")
    live_counts = counts[0]
    my_count = jnp.sum(
        jnp.where(jnp.arange(row_count, dtype=jnp.int32) == row_index, live_counts, 0)
    )
    keep_slot = (jnp.arange(slot_count, dtype=jnp.int32) < my_count)[:, None]
    gathered_kv, gathered_hyper = side_by_side((kv_rows, hyper_rows), "row", 0, 1)
    block_pixels = pixel_count // row_count
    pieces = several_exchanges(
        tile_flat.reshape(row_count, block_pixels, model_width), "row", 2, 0, 0
    )
    pix_block = row_index * block_pixels + jnp.arange(block_pixels, dtype=jnp.int32)
    block_keys = (
        pieces.astype(jnp.float32) + dense_pe(pix_block, grid_side, pe_gauss)[None]
    ).astype(jnp.bfloat16)
    block_query = jnp.dot(block_keys, query_weight, preferred_element_type=jnp.float32).astype(
        jnp.bfloat16
    )
    mean_count = slot_count // 3
    packed_total = mean_count * row_count
    count_ends = jnp.cumsum(live_counts)
    count_starts = count_ends - live_counts
    packed_order = jnp.arange(packed_total, dtype=jnp.int32)
    tile_of = jnp.sum((packed_order[:, None] >= count_ends[None, :]).astype(jnp.int32), axis=1)
    owner_hot = tile_of[:, None] == jnp.arange(row_count, dtype=jnp.int32)[None, :]
    slot_of = packed_order - jnp.sum(jnp.where(owner_hot, count_starts[None, :], 0), axis=1)
    source_row = tile_of * slot_count + slot_of

    def one_block(packed_ids):
        tile_ids, row_ids = packed_ids
        return image_side(
            pieces[tile_ids],
            block_query[tile_ids],
            gathered_kv[row_ids],
            gathered_hyper[row_ids],
            i2t_out,
            ln_gains[3],
        )

    logits = lax.map(
        one_block,
        (tile_of.reshape(mean_count, row_count), source_row.reshape(mean_count, row_count)),
    )
    logits = logits.reshape(packed_total, block_pixels)
    outgoing = (
        jnp.zeros((slot_count, row_count, block_pixels), jnp.bfloat16)
        .at[slot_of, tile_of]
        .set(logits)
    )
    returned = lax.all_to_all(outgoing, "row", split_axis=1, concat_axis=1, tiled=True)
    mask_logits = returned.reshape(slot_count, pixel_count)
    coverage = jnp.sum(
        jnp.where(keep_slot, jax.nn.sigmoid(mask_logits.astype(jnp.float32)), 0.0), axis=0
    ).reshape(grid_side, grid_side)
    padded = padded_2(coverage, (("col", 1),), SEAM)
    blended = jnp.zeros_like(coverage)
    for offset in range(-SEAM, SEAM + 1):
        factor = (SEAM + 1 - abs(offset)) / (SEAM + 1) ** 2
        blended = blended + factor * padded[:, SEAM + offset : SEAM + offset + grid_side]
    return (mask_logits.reshape(1, 1, slot_count, pixel_count), blended)


def solution(mesh):
    placed = (
        P("row", "col", None),
        P("col", None),
        P("row", "col", None, None),
        P(),
        P(),
        P(),
        P(),
        P(),
        P(),
        P(),
        P(),
        P(),
        P(),
        P(),
        P(),
        P(),
    )
    return jax.shard_map(
        shards,
        mesh=mesh,
        in_specs=placed,
        out_specs=(P("row", "col", None, None), P("row", "col")),
        check_vma=False,
    )
```

profile of v0, /device:TPU:97, one launch (start us, length us, event | category | flops | bytes accessed | tf_op | source)
XLA Modules:
  0.0 483.2 jit_solution(1258931719096998958)
XLA Ops:
  0.6 3.2 fusion.113
  3.9 6.9 %all-to-all-start = ((bf16[16,1,128,256]{3,2,1,0:T(8,128)(2,1)}), bf16[16,1,128,256]{3,2,1,0:T(8,128)(2,1)}, u32[]{:S(2)}, u32[]{:S(2)}) async-start(bf16[16,1,128,256]{3,2,1,0:T(8,128)(2,1)} %get-tuple-element.205), calls=%async_computation | async-start | bytes 2097152 | tf_op jit(solution)/shard_map/all_to_all | solution.py:63
  14.6 3.3 fusion.117
  18.6 3.5 convolution_bitcast_fusion
  27.1 2.9 fusion.61
  30.0 9.4 %fusion.23 = (f32[4096,128]{1,0:T(8,128)}, f32[4096,128]{1,0:T(8,128)}) fusion(f32[128]{0:T(128)S(1)} %copy-done.19, f32[4096]{0:T(1024)S(1)} %copy-done.13, f32[128]{0:T(128)S(1)} %copy-done.17, f32[4096]{0:T(1024)S(1)} %get-tuple-element.233), kind=kLoop, calls=%fused_computation.57 | loop fusion | flops 2097152 | bytes 4228096 | tf_op jit(solution)/shard_map/sin | solution.py:104
  39.4 8.5 %convolution_multiply_fusion.1 = f32[768,4096]{1,0:T(8,128)} fusion(f32[4096,128]{1,0:T(8,128)} %get-tuple-element.211, f32[4096,128]{1,0:T(8,128)} %get-tuple-element.210, bf16[4096,256]{1,0:T(8,128)(2,1)S(1)} %bitcast.176, pred[8,128]{1,0:T(8,128)(4,1)S(1)} %iota_compare_fusion.2, bf16[96,128]{1,0:T(8,128)(2,1)S(1)} %bitcast.184, bf16[256,384]{1,0:T(8,128)(2,1)} %param.26), kind=kOutput, calls=%fused_computation.46 | convolution fusion | flops 1081704448 | bytes 18965504 | tf_op jit(solution)/shard_map/dot_general | solution.py:171
  47.8 8.3 %online-softmax = f32[768,128]{1,0:T(8,128)} custom-call(f32[768,4096]{1,0:T(8,128)} %convolution_multiply_fusion.1, f32[4096,128]{1,0:T(8,128)} %fusion.61), custom_call_target="tpu_custom_call" | custom-call | tf_op online-softmax
  60.3 6.6 %all-to-all-start.1 = ((bf16[16,1,128,256]{3,2,1,0:T(8,128)(2,1)}), bf16[16,1,128,256]{3,2,1,0:T(8,128)(2,1)S(1)}, u32[]{:S(2)}, u32[]{:S(2)}) async-start(bf16[16,1,128,256]{3,2,1,0:T(8,128)(2,1)} %get-tuple-element.206), calls=%async_computation.1 | async-start | bytes 2097152 | tf_op jit(solution)/shard_map/all_to_all | solution.py:63
  68.0 14.4 %all-to-all-done.1 = bf16[16,1,128,256]{3,2,1,0:T(8,128)(2,1)S(1)} async-done(((bf16[16,1,128,256]{3,2,1,0:T(8,128)(2,1)}), bf16[16,1,128,256]{3,2,1,0:T(8,128)(2,1)S(1)}, u32[]{:S(2)}, u32[]{:S(2)}) %all-to-all-start.1) | async-done | bytes 1048608 | tf_op jit(solution)/shard_map/all_to_all | solution.py:63
  83.4 4.6 all-to-all-start.2
  88.6 2.7 maximum_bitcast_fusion
  93.3 11.0 %all-to-all-done.2 = bf16[16,48,768]{2,1,0:T(8,128)(2,1)} async-done(((bf16[16,48,768]{2,1,0:T(8,128)(2,1)}), bf16[16,48,768]{2,1,0:T(8,128)(2,1)}, u32[]{:S(2)}, u32[]{:S(2)}) %all-to-all-start.2) | async-done | bytes 1179680 | tf_op jit(solution)/shard_map/all_to_all | solution.py:19
  108.3 331.9 %while.12 = (s32[]{:T(128)}, bf16[16,16,256]{2,1,0:T(8,128)(2,1)S(1)}, s32[16,16]{1,0:T(8,128)S(1)}, bf16[16,256,256]{2,1,0:T(8,128)(2,1)}, s32[16,16]{1,0:T(8,1...) while((s32[]{:T(128)}, ...), condition=%wide.region_18.19_spmd, body=%wide.region_14.18_spmd.sunk | while | flops 1090040960 | bytes 60195656 | solution.py:305
  111.5 2.6 fusion.138
  118.8 3.0 fusion.139
  126.1 2.9 multiply_reduce_fusion.8
  132.2 2.6 fusion.138
  139.6 3.0 fusion.139
  146.9 2.9 multiply_reduce_fusion.8
  153.0 2.6 fusion.138
  160.3 3.0 fusion.139
  167.6 2.9 multiply_reduce_fusion.8
  173.7 2.6 fusion.138
  181.1 3.0 fusion.139
  188.4 2.9 multiply_reduce_fusion.8
  194.5 2.6 fusion.138
  201.8 3.0 fusion.139
  209.1 2.9 multiply_reduce_fusion.8
  215.2 2.6 fusion.138
  222.5 3.0 fusion.139
  229.8 2.9 multiply_reduce_fusion.8
  243.3 3.0 fusion.139
  250.6 2.9 multiply_reduce_fusion.8
  256.7 2.6 fusion.138
  264.0 3.0 fusion.139
  271.3 2.9 multiply_reduce_fusion.8
  277.4 2.6 fusion.138
  284.8 3.0 fusion.139
  292.1 2.9 multiply_reduce_fusion.8
  298.2 2.6 fusion.138
  305.5 3.0 fusion.139
  312.8 2.9 multiply_reduce_fusion.8
  318.9 2.6 fusion.138
  326.3 3.0 fusion.139
  333.6 2.9 multiply_reduce_fusion.8
  339.7 2.6 fusion.138
  347.0 3.0 fusion.139
  354.3 2.9 multiply_reduce_fusion.8
  367.8 3.0 fusion.139
  375.1 2.9 multiply_reduce_fusion.8
  381.2 2.6 fusion.138
  388.5 3.0 fusion.139
  395.8 2.9 multiply_reduce_fusion.8
  409.3 3.0 fusion.139
  416.6 2.9 multiply_reduce_fusion.8
  422.7 2.6 fusion.138
  430.0 3.0 fusion.139
  437.3 2.9 multiply_reduce_fusion.8
  440.3 13.0 %scatter_fusion = bf16[48,16,256]{2,1,0:T(8,128)(2,1)S(1)} fusion(bf16[48,16,256]{2,1,0:T(8,128)(2,1)S(1)} %broadcast_in_dim.67, s32[256]{0:T(256)S(1)} %bitcast.177, bf16[256,256]{1,0:T(8,128)(2,1)S(1)} %bitcast.182), kind=kCustom, calls=%fused_computation.4 | custom fusion | bytes 395264 | tf_op jit(solution)/shard_map/scatter | solution.py:313
  454.2 4.3 all-to-all-start.3
  459.7 7.1 %all-to-all-done.3 = bf16[48,16,256]{2,0,1:T(8,128)(2,1)S(1)} async-done(((bf16[48,16,256]{2,0,1:T(8,128)(2,1)}), bf16[48,16,256]{2,0,1:T(8,128)(2,1)S(1)}, u32[]{:S(2)}, u32[]{:S(2)}) %all-to-all-start.3) | async-done | bytes 393248 | tf_op jit(solution)/shard_map/all_to_all | solution.py:315
  467.2 8.8 %collective-permute-start = (f32[64,4]{1,0:T(8,128)S(1)}, f32[64,4]{1,0:T(8,128)S(1)}, u32[]{:S(2)}, u32[]{:S(2)}) collective-permute-start(f32[64,4]{1,0:T(8,128)S(1)} %get-tuple-element.212), channel_id=1, source_target_pairs={{0,1},{1,2},{2,3},{3,4},{4,5},{5,6},{6,7},{7,8},{8,9},{9,10},{10,1... | collective-permute-start | bytes 3080 | tf_op jit(solution)/shard_map/ppermute | solution.py:75
  479.0 3.5 collective-permute-done.1
  (503 shorter events, 228.9 us)
Async XLA Ops:
  0.6 57.2 %copy-start = (bf16[256,2048]{1,0:T(8,128)(2,1)S(1)}, bf16[256,2048]{1,0:T(8,128)(2,1)}, u32[]{:S(2)}) copy-start(bf16[256,2048]{1,0:T(8,128)(2,1)} %param.28) | copy-start | bytes 3145732
  3.9 8.1 %copy-start.22 = (f32[2,128]{1,0:T(2,128)S(1)}, f32[2,128]{1,0:T(2,128)}, u32[]{:S(2)}) copy-start(f32[2,128]{1,0:T(2,128)} %param.21) | copy-start | bytes 3076
  3.9 8.1 %copy-start.23 = (s32[1,1,2,48]{3,2,1,0:T(2,128)S(1)}, s32[1,1,2,48]{3,2,1,0:T(2,128)}, u32[]{:S(2)}) copy-start(s32[1,1,2,48]{3,2,1,0:T(2,128)} %param.20) | copy-start | bytes 1156
  3.9 8.7 %copy-start.20 = (f32[256]{0:T(256)S(1)}, f32[256]{0:T(256)}, u32[]{:S(2)}) copy-start(f32[256]{0:T(256)} %param.22) | copy-start | bytes 3076
  3.9 8.7 %copy-start.21 = (f32[256]{0:T(256)S(1)}, f32[256]{0:T(256)}, u32[]{:S(2)}) copy-start(f32[256]{0:T(256)} %param.23) | copy-start | bytes 3076
  3.9 10.0 %copy-start.10 = (bf16[256,768]{1,0:T(8,128)(2,1)S(1)}, bf16[256,768]{1,0:T(8,128)(2,1)}, u32[]{:S(2)}) copy-start(bf16[256,768]{1,0:T(8,128)(2,1)} %param.24) | copy-start | bytes 1179652
  3.9 56.4 %all-to-all-start = ((bf16[16,1,128,256]{3,2,1,0:T(8,128)(2,1)}), bf16[16,1,128,256]{3,2,1,0:T(8,128)(2,1)}, u32[]{:S(2)}, u32[]{:S(2)}) async-start(bf16[16,1,128,256]{3,2,1,0:T(8,128)(2,1)} %get-tuple-element.205), calls=%async_computation | async-start | bytes 2097152 | tf_op jit(solution)/shard_map/all_to_all | solution.py:63
  18.6 8.4 %copy-start.2 = (bf16[64,64,256]{2,1,0:T(8,128)(2,1)S(1)}, bf16[64,64,256]{2,1,0:T(8,128)(2,1)}, u32[]{:S(2)}) copy-start(bf16[64,64,256]{2,1,0:T(8,128)(2,1)} %param.18) | copy-start | bytes 6291460
  27.1 2.9 copy-start.13
  27.1 2.9 copy-start.17
  27.1 2.9 copy-start.19
  47.8 9.5 %copy-start.14 = (bf16[128,256]{1,0:T(8,128)(2,1)S(1)}, bf16[128,256]{1,0:T(8,128)(2,1)}, u32[]{:S(2)}) copy-start(bf16[128,256]{1,0:T(8,128)(2,1)} %param.27) | copy-start | bytes 196612
  56.1 2.4 copy-start.5
  57.8 2.1 copy-start.7
  57.8 2.1 copy-start.9
  57.8 2.1 copy-start.12
  58.5 8.4 %copy-start.11 = (bf16[2,256,256]{2,1,0:T(8,128)(2,1)S(1)}, bf16[2,256,256]{2,1,0:T(8,128)(2,1)}, u32[]{:S(2)}) copy-start(bf16[2,256,256]{2,1,0:T(8,128)(2,1)} %param.32) | copy-start | bytes 786436
  60.3 22.0 %all-to-all-start.1 = ((bf16[16,1,128,256]{3,2,1,0:T(8,128)(2,1)}), bf16[16,1,128,256]{3,2,1,0:T(8,128)(2,1)S(1)}, u32[]{:S(2)}, u32[]{:S(2)}) async-start(bf16[16,1,128,256]{3,2,1,0:T(8,128)(2,1)} %get-tuple-element.206), calls=%async_computation.1 | async-start | bytes 2097152 | tf_op jit(solution)/shard_map/all_to_all | solution.py:63
  67.1 21.3 %copy-start.15 = (bf16[128,256]{1,0:T(8,128)(2,1)S(1)}, bf16[128,256]{1,0:T(8,128)(2,1)}, u32[]{:S(2)}) copy-start(bf16[128,256]{1,0:T(8,128)(2,1)} %param.31) | copy-start | bytes 196612
  83.4 20.9 %all-to-all-start.2 = ((bf16[16,48,768]{2,1,0:T(8,128)(2,1)}), bf16[16,48,768]{2,1,0:T(8,128)(2,1)}, u32[]{:S(2)}, u32[]{:S(2)}) async-start(bf16[16,48,768]{2,1,0:T(8,128)(2,1)} %broadcast_in_dim.90), calls=%async_computation.2 | async-start | bytes 2359296 | tf_op jit(solution)/shard_map/all_to_all | solution.py:19
  108.3 3.1 copy-start.3
  121.9 1.9 copy-start.1
  126.1 2.9 copy-start.4
  129.1 3.1 copy-start.3
  142.6 1.9 copy-start.1
  146.9 2.9 copy-start.4
  149.8 3.1 copy-start.3
  163.3 1.9 copy-start.1
  167.6 2.9 copy-start.4
  170.6 3.1 copy-start.3
  184.1 1.9 copy-start.1
  188.4 2.9 copy-start.4
  191.3 3.1 copy-start.3
  209.1 2.9 copy-start.4
  212.1 3.1 copy-start.3
  229.8 2.9 copy-start.4
  232.8 3.1 copy-start.3
  246.3 1.9 copy-start.1
  250.6 2.9 copy-start.4
  253.5 3.1 copy-start.3
  267.1 1.9 copy-start.1
  271.3 2.9 copy-start.4
  274.3 3.1 copy-start.3
  287.8 1.9 copy-start.1
  292.1 2.9 copy-start.4
  295.0 3.1 copy-start.3
  312.8 2.9 copy-start.4
  315.8 3.1 copy-start.3
  333.6 2.9 copy-start.4
  336.5 3.1 copy-start.3
  354.3 2.9 copy-start.4
  357.3 3.1 copy-start.3
  375.1 2.9 copy-start.4
  378.0 3.1 copy-start.3
  391.5 1.9 copy-start.1
  395.8 2.9 copy-start.4
  398.8 3.1 copy-start.3
  412.3 1.9 copy-start.1
  416.6 2.9 copy-start.4
  419.5 3.1 copy-start.3
  437.3 2.9 copy-start.4
  454.2 12.7 %all-to-all-start.3 = ((bf16[48,16,256]{2,0,1:T(8,128)(2,1)}), bf16[48,16,256]{2,0,1:T(8,128)(2,1)S(1)}, u32[]{:S(2)}, u32[]{:S(2)}) async-start(bf16[48,16,256]{2,0,1:T(8,128)(2,1)} %copy.70), calls=%async_computation.3 | async-start | bytes 786432 | tf_op jit(solution)/shard_map/all_to_all | solution.py:315
  467.2 11.8 %collective-permute-start = (f32[64,4]{1,0:T(8,128)S(1)}, f32[64,4]{1,0:T(8,128)S(1)}, u32[]{:S(2)}, u32[]{:S(2)}) collective-permute-start(f32[64,4]{1,0:T(8,128)S(1)} %get-tuple-element.212), channel_id=1, source_target_pairs={{0,1},{1,2},{2,3},{3,4},{4,5},{5,6},{6,7},{7,8},{8,9},{9,10},{10,1... | collective-permute-start | bytes 3080 | tf_op jit(solution)/shard_map/ppermute | solution.py:75
  476.0 6.4 %collective-permute-start.1 = (f32[64,4]{1,0:T(8,128)S(1)}, f32[64,4]{1,0:T(8,128)S(1)}, u32[]{:S(2)}, u32[]{:S(2)}) collective-permute-start(f32[64,4]{1,0:T(8,128)S(1)} %get-tuple-element.213), channel_id=1, source_target_pairs={{1,0},{2,1},{3,2},{4,3},{5,4},{6,5},{7,6},{8,7},{9,8},{10,9},{11,1... | collective-permute-start | bytes 3080 | tf_op jit(solution)/shard_map/ppermute | solution.py:77
  (12 other events, 17.6 us)
where the time goes:
time: 486 us; the launch traced here: 483 us
  local copies, waits for them, and re-layouts  208 us (43%)
  matrix products  115 us (24%)
  other arithmetic  78.3 us (16%)
  waiting for transfers between devices  35.9 us (7%)
  starting transfers between devices  33.2 us (7%)
  Pallas kernels  8.27 us (2%)
    gather x32, local copies, waits for them, and re-layouts, one_block(): pieces[tile_ids]  75.2 us
    dot_general x16, matrix products, image_side(): jnp.einsum('bpi,id->bpd', mixture, out_weight, preferred_element_type=jnp...  48.4 us
    reduce_sum x16, other arithmetic, image_side(): jnp.sum(normed * hyper_rows.astype(jnp.float32)[:, None, :], axis=-1)  46.3 us
    dot_general x16, matrix products, image_side(): jnp.dot(products.reshape(batch_rows * pix_rows, inner_width), same_head,...  41.8 us
    gather x16, local copies, waits for them, and re-layouts, one_block(): gathered_kv[row_ids]  33.2 us
    gather x16, local copies, waits for them, and re-layouts, one_block(): gathered_hyper[row_ids]  26 us
    while x96, local copies, waits for them, and re-layouts  23.4 us
    all_to_all x2, waiting for transfers between devices, several_exchanges(): lax.all_to_all(slab, axis, split_axis=0, concat_axis=0, tiled=True)  14.4 us
  transfers between devices with their start and end apart: 6, of which 4 were waited for; matrix products, arithmetic and copies ran while one was open for 10% of the time, Pallas kernels for 2%

commit v1 on v0

v1 whole, which is shorter than its diff:
```python
import functools
import math

import jax
import jax.numpy as jnp
import numpy as np
from jax import lax
from jax.experimental import pallas as pl
from jax.experimental.pallas import tpu as pltpu
from jax.sharding import PartitionSpec as P

HEADS = 8
SEAM = 4
IMG = 1024
EPS = 1e-05
F32 = jnp.float32
BF16 = jnp.bfloat16
LANES = 128
CHUNK = 512
GROUP = 16


def turn_polynomials():
    z = np.linspace(0.0, 0.25, 4001)[1:]
    r = np.sqrt(z)
    fit = np.polynomial.chebyshev.Chebyshev.fit
    power = lambda c: [float(v) for v in c.convert(kind=np.polynomial.Polynomial, domain=[-1, 1]).coef]
    return (
        power(fit(z, np.sin(2 * math.pi * r) / r, 8, domain=[0.0, 0.25])),
        power(fit(z, np.cos(2 * math.pi * r), 8, domain=[0.0, 0.25])),
    )


SIN_COEF, COS_COEF = turn_polynomials()


def sin_cos_turns(turns):
    r = turns - jnp.floor(turns + 0.5)
    z = r * r
    s = jnp.full_like(z, SIN_COEF[-1])
    c = jnp.full_like(z, COS_COEF[-1])
    for a, b in zip(SIN_COEF[-2::-1], COS_COEF[-2::-1]):
        s = s * z + a
        c = c * z + b
    return s * r, c


def dot(a, b):
    return lax.dot_general(a, b, (((1,), (0,)), ((), ())), preferred_element_type=F32)


def dot_t(a, b):
    return lax.dot_general(a, b, (((1,), (1,)), ((), ())), preferred_element_type=F32)


def halves(values):
    high = values.astype(BF16)
    return high, (values - high.astype(F32)).astype(BF16)


def weight_dot(values, weight):
    rows = values.shape[0]
    both = dot(jnp.concatenate(halves(values), axis=0), weight)
    return both[:rows] + both[rows:]


def layer_norm(values, gain):
    centred = values - jnp.mean(values, axis=-1, keepdims=True)
    var = jnp.mean(centred * centred, axis=-1, keepdims=True)
    return centred * lax.rsqrt(var + EPS) * gain


def rounded(values):
    return values.astype(BF16).astype(F32)


def by_head(values):
    lane = lax.broadcasted_iota(jnp.int32, values.shape, 1) // (values.shape[1] // HEADS)
    return jnp.concatenate([jnp.where(lane == h, values, 0.0) for h in range(HEADS)], axis=0)


def centred_rows(values):
    return values - jnp.mean(values, axis=-1, keepdims=True)


def as_column(row):
    n = row.shape[1]
    i = lax.broadcasted_iota(jnp.int32, (n, n), 0)
    j = lax.broadcasted_iota(jnp.int32, (n, n), 1)
    return jnp.sum(jnp.where(i == j, jnp.broadcast_to(row, (n, n)), 0.0), axis=1, keepdims=True)


def tile_kernel(
    counts_ref,
    emb_ref,
    points_ref,
    gauss_ref,
    prompt_ref,
    mask_ref,
    sa_qkv_ref,
    sa_out_ref,
    t2i_ref,
    t2i_out_ref,
    up_ref,
    down_ref,
    i2t_ref,
    i2t_out_ref,
    hyper_ref,
    gains_ref,
    logits_ref,
    cov_ref,
    keys_ref,
    sq_ref,
    table_ref,
    score_ref,
    aq_ref,
    top_ref,
    sum_ref,
    acc_ref,
    gap_ref,
    row_ref,
    coef_ref,
    t_ref,
    r_ref,
):
    cells, width = emb_ref.shape
    slots = points_ref.shape[1]
    tokens = 2 * slots
    half = width // 2
    inner = t2i_ref.shape[1] // 3
    side = math.isqrt(cells)
    chunks = cells // CHUNK
    count = counts_ref[0, lax.axis_index("row")]

    steps = (2.0 * (lax.broadcasted_iota(jnp.int32, (side, half), 0).astype(F32) + 0.5)) / side - 1.0
    sin_x, cos_x = sin_cos_turns(steps * gauss_ref[0:1, :])
    sin_y, cos_y = sin_cos_turns(steps * gauss_ref[1:2, :])
    table_ref[0] = sin_y
    table_ref[1] = cos_y

    def cell_body(y, carry):
        at = pl.multiple_of(y * side, side)
        e = emb_ref[pl.ds(at, side), :].astype(F32)
        sy = table_ref[0, pl.ds(y, 1), :]
        cy = table_ref[1, pl.ds(y, 1), :]
        e1, e2 = e[:, :half], e[:, half:]
        keys_ref[pl.ds(at, side), :half] = (e1 + (sin_x * cy + cos_x * sy)).astype(BF16)
        keys_ref[pl.ds(at, side), half:] = (e2 + (cos_x * cy - sin_x * sy)).astype(BF16)
        high, low = halves(e1 * e1 + e2 * e2)
        sq_ref[pl.ds(at, side), :half] = high
        sq_ref[pl.ds(at, side), half:] = low
        return carry

    lax.fori_loop(0, side, cell_body, 0)

    coords = (2.0 * (points_ref[...].astype(F32) + 0.5)) / IMG - 1.0
    turns = as_column(coords[0:1, :]) * gauss_ref[0:1, :] + as_column(coords[1:2, :]) * gauss_ref[1:2, :]
    sin_p, cos_p = sin_cos_turns(turns)
    prompt = jnp.concatenate([sin_p, cos_p], axis=1) + prompt_ref[...]
    start = jnp.concatenate([jnp.broadcast_to(mask_ref[...], (slots, width)), prompt], axis=0)
    qkv = weight_dot(start, sa_qkv_ref[...])
    q, k, v = qkv[:, :width], qkv[:, width : 2 * width], qkv[:, 2 * width :]
    k_gap = k[slots:] - k[:slots]
    v_gap = v[slots:] - v[:slots]
    self_width = width // HEADS
    i = lax.broadcasted_iota(jnp.int32, (width, width), 0) // self_width
    j = lax.broadcasted_iota(jnp.int32, (width, width), 1) // self_width
    same = jnp.where(i == j, 1.0, 0.0).astype(BF16)
    gap = weight_dot(q * jnp.concatenate([k_gap, k_gap], axis=0), same) / math.sqrt(self_width)
    second = jax.nn.sigmoid(gap)
    joined = jnp.concatenate([v[:slots], v[:slots]], axis=0) + second * jnp.concatenate([v_gap, v_gap], axis=0)
    queries = layer_norm(weight_dot(joined, sa_out_ref[...]), gains_ref[0:1, :])
    cross_q = rounded(weight_dot(queries + start, t2i_ref[:, :inner]))
    scale = math.log2(math.e) / math.sqrt(inner // HEADS)
    aq_ref[...] = (dot_t(by_head(cross_q).astype(BF16), t2i_ref[:, inner : 2 * inner]) * scale).astype(BF16)

    top_ref[...] = jnp.full(top_ref.shape, -jnp.inf, F32)

    def score_body(c, carry):
        at = pl.multiple_of(c * CHUNK, CHUNK)
        s = dot_t(aq_ref[...], keys_ref[pl.ds(at, CHUNK), :])
        score_ref[:, pl.ds(at, CHUNK)] = s
        top = top_ref[...]
        for k0 in range(0, CHUNK, LANES):
            top = jnp.maximum(top, s[:, k0 : k0 + LANES])
        top_ref[...] = top
        return carry

    lax.fori_loop(0, chunks, score_body, 0)
    top_ref[...] = jnp.broadcast_to(jnp.max(top_ref[...], axis=1, keepdims=True), top_ref.shape)
    sum_ref[...] = jnp.zeros_like(sum_ref)
    acc_ref[...] = jnp.zeros_like(acc_ref)

    def prob_body(c, carry):
        at = pl.multiple_of(c * CHUNK, CHUNK)
        top = top_ref[...]
        total = sum_ref[...]
        parts = []
        for k0 in range(0, CHUNK, LANES):
            p = jnp.exp2(score_ref[:, pl.ds(pl.multiple_of(at + k0, LANES), LANES)] - top)
            total = total + p
            parts.append(p.astype(BF16))
        sum_ref[...] = total
        acc_ref[...] += dot(jnp.concatenate(parts, axis=1), emb_ref[pl.ds(at, CHUNK), :])
        return carry

    lax.fori_loop(0, chunks, prob_body, 0)
    mean_cell = acc_ref[...] / jnp.sum(sum_ref[...], axis=1, keepdims=True)
    head_out = dot(mean_cell.astype(BF16), t2i_ref[:, 2 * inner :])
    lane = lax.broadcasted_iota(jnp.int32, (tokens, inner), 1) // (inner // HEADS)
    cross_out = jnp.zeros((tokens, inner), F32)
    for h in range(HEADS):
        cross_out = jnp.where(lane == h, head_out[h * tokens : (h + 1) * tokens], cross_out)

    queries = layer_norm(queries + weight_dot(cross_out, t2i_out_ref[...]), gains_ref[1:2, :])
    hidden = jnp.maximum(weight_dot(queries, up_ref[...]), 0.0)
    queries = layer_norm(queries + weight_dot(hidden, down_ref[...]), gains_ref[2:3, :])
    back_k = rounded(weight_dot(queries + start, i2t_ref[:, inner : 2 * inner]))
    back_v = rounded(weight_dot(queries, i2t_ref[:, 2 * inner :]))
    hyper = rounded(weight_dot(jnp.maximum(weight_dot(queries[:slots], hyper_ref[0]), 0.0), hyper_ref[1]))

    key_gap = back_k[:slots] - back_k[slots:]
    gap_scale = 0.5 / math.sqrt(inner // HEADS)
    gap_ref[...] = (dot_t(by_head(key_gap).astype(BF16), i2t_ref[:, :inner]) * gap_scale).astype(BF16)
    spread = 0.5 * (back_v[:slots] - back_v[slots:])
    middle = 0.5 * (back_v[:slots] + back_v[slots:])
    u = rounded(centred_rows(dot(by_head(spread).astype(BF16), i2t_out_ref[...])))
    b = rounded(centred_rows(weight_dot(middle, i2t_out_ref[...])))
    g = rounded(centred_rows(hyper * gains_ref[3:4, :]))
    heads = HEADS * slots
    row_ref[:heads, :] = (2.0 * u).astype(BF16)
    row_ref[heads : heads + slots, :] = (2.0 * b).astype(BF16)
    row_ref[heads + slots : heads + 2 * slots, :] = g.astype(BF16)
    row_ref[heads + 2 * slots :, :] = jnp.ones((row_ref.shape[0] - heads - 2 * slots, width), BF16)

    def product(left, right, factor):
        value = jnp.sum(left * right, axis=1, keepdims=True) * factor
        return jnp.broadcast_to(value, (slots, LANES))

    us = [u[h * slots : (h + 1) * slots] for h in range(HEADS)]
    n = 0
    for h in range(HEADS):
        for h2 in range(h + 1):
            coef_ref[n] = product(us[h], us[h2], 1.0 if h == h2 else 2.0)
            n += 1
    for h in range(HEADS):
        coef_ref[n + h] = product(us[h], b, 2.0)
        coef_ref[n + HEADS + h] = product(us[h], g, 1.0)
    n += 2 * HEADS
    coef_ref[n] = product(b, b, 1.0)
    coef_ref[n + 1] = product(b, g, 1.0)

    ones = jnp.ones((GROUP, width), BF16)

    def image_body(c, carry):
        at = pl.multiple_of(c * CHUNK, CHUNK)
        t_ref[...] = jnp.tanh(dot_t(gap_ref[...], keys_ref[pl.ds(at, CHUNK), :]))
        r_ref[...] = dot_t(row_ref[...], emb_ref[pl.ds(at, CHUNK), :])
        squares = dot_t(ones, sq_ref[pl.ds(at, CHUNK), :])
        for k0 in range(0, CHUNK, LANES):
            lanes = slice(k0, k0 + LANES)
            sums = r_ref[heads + 2 * slots :, lanes]
            own = squares[:, lanes] - sums * sums * (1.0 / width)
            cover = jnp.zeros((8, LANES), F32)
            for s0 in range(0, slots, GROUP):
                rows = slice(s0, s0 + GROUP)
                ts = [t_ref[h * slots + s0 : h * slots + s0 + GROUP, lanes] for h in range(HEADS)]
                var = own + r_ref[heads + s0 : heads + s0 + GROUP, lanes] + coef_ref[n, rows]
                out = r_ref[heads + slots + s0 : heads + slots + s0 + GROUP, lanes] + coef_ref[n + 1, rows]
                m = 0
                for h in range(HEADS):
                    line = r_ref[h * slots + s0 : h * slots + s0 + GROUP, lanes] + coef_ref[n - 2 * HEADS + h, rows]
                    for h2 in range(h + 1):
                        line = line + ts[h2] * coef_ref[m, rows]
                        m += 1
                    var = var + ts[h] * line
                    out = out + ts[h] * coef_ref[n - HEADS + h, rows]
                var = jnp.maximum(var, 0.0)
                logit = (out * lax.rsqrt(var + EPS * width)).astype(BF16)
                live = lax.broadcasted_iota(jnp.int32, (GROUP, LANES), 0) + s0 < count
                masked = jnp.where(live, logit.astype(F32), 0.0)
                logits_ref[rows, pl.ds(pl.multiple_of(at + k0, LANES), LANES)] = masked.astype(BF16)
                sig = jnp.where(live, jax.nn.sigmoid(masked), 0.0)
                cover = cover + (sig[:8] + sig[8:])
            cov_ref[pl.ds(c * (CHUNK // LANES) + k0 // LANES, 1), :] = jnp.sum(cover, axis=0, keepdims=True)
        return carry

    lax.fori_loop(0, chunks, image_body, 0)


def seam_kernel(n, cov_ref, out_ref, left_ref, right_ref, send_sem, recv_sem):
    me = lax.axis_index("col")
    side = out_ref.shape[0]
    has_left, has_right = me > 0, me < n - 1
    barrier = pltpu.get_barrier_semaphore()
    mesh_id = pl.DeviceIdType.MESH

    def to_left():
        return pltpu.make_async_remote_copy(
            src_ref=cov_ref,
            dst_ref=right_ref,
            send_sem=send_sem.at[0],
            recv_sem=recv_sem.at[0],
            device_id={"col": me - 1},
            device_id_type=mesh_id,
        )

    def to_right():
        return pltpu.make_async_remote_copy(
            src_ref=cov_ref,
            dst_ref=left_ref,
            send_sem=send_sem.at[1],
            recv_sem=recv_sem.at[1],
            device_id={"col": me + 1},
            device_id_type=mesh_id,
        )

    @pl.when(has_left)
    def _():
        pl.semaphore_signal(barrier, inc=1, device_id={"col": me - 1}, device_id_type=mesh_id)

    @pl.when(has_right)
    def _():
        pl.semaphore_signal(barrier, inc=1, device_id={"col": me + 1}, device_id_type=mesh_id)

    pl.semaphore_wait(barrier, has_left.astype(jnp.int32) + has_right.astype(jnp.int32))

    @pl.when(has_left)
    def _():
        to_left().start()

    @pl.when(has_right)
    def _():
        to_right().start()

    cov = cov_ref[...]
    x = lax.broadcasted_iota(jnp.int32, cov.shape, 1) % side
    total = (SEAM + 1.0) * cov
    for d in range(1, SEAM + 1):
        inside = jnp.where(x < side - d, pltpu.roll(cov, LANES - d, 1), 0.0)
        inside = inside + jnp.where(x >= d, pltpu.roll(cov, d, 1), 0.0)
        total = total + (SEAM + 1.0 - d) * inside

    @pl.when(jnp.logical_not(has_left))
    def _():
        left_ref[...] = jnp.zeros_like(left_ref)

    @pl.when(jnp.logical_not(has_right))
    def _():
        right_ref[...] = jnp.zeros_like(right_ref)

    @pl.when(has_right)
    def _():
        to_right().wait_send()
        to_left().wait_recv()

    @pl.when(has_left)
    def _():
        to_left().wait_send()
        to_right().wait_recv()

    left, right = left_ref[...], right_ref[...]
    for d in range(1, SEAM + 1):
        outside = jnp.where(x >= side - d, pltpu.roll(right, side - d, 1), 0.0)
        outside = outside + jnp.where(x < d, pltpu.roll(left, side + d, 1), 0.0)
        total = total + (SEAM + 1.0 - d) * outside
    total = total * (1.0 / (SEAM + 1) ** 2)
    out_ref[pl.ds(0, side // 2, stride=2), :] = total[:, :side]
    out_ref[pl.ds(1, side // 2, stride=2), :] = total[:, side:]


def tile_call(counts, emb, points, gauss, prompt, mask, sa_qkv, sa_out, t2i, t2i_out, up, down, i2t, i2t_out, hyper, gains):
    cells, width = emb.shape
    slots = points.shape[1]
    rows = 2 * slots * HEADS
    half = width // 2
    heads = slots * HEADS
    products = HEADS * (HEADS + 1) // 2 + 2 * HEADS + 2
    vmem = pl.BlockSpec(memory_space=pltpu.VMEM)
    return pl.pallas_call(
        tile_kernel,
        out_shape=(
            jax.ShapeDtypeStruct((slots, cells), BF16),
            jax.ShapeDtypeStruct((cells // LANES, LANES), F32),
        ),
        in_specs=[pl.BlockSpec(memory_space=pltpu.SMEM)] + [vmem] * 15,
        out_specs=(vmem, vmem),
        scratch_shapes=[
            pltpu.VMEM((cells, width), BF16),
            pltpu.VMEM((cells, width), BF16),
            pltpu.VMEM((2, math.isqrt(cells), half), F32),
            pltpu.VMEM((rows, cells), F32),
            pltpu.VMEM((rows, width), BF16),
            pltpu.VMEM((rows, LANES), F32),
            pltpu.VMEM((rows, LANES), F32),
            pltpu.VMEM((rows, width), F32),
            pltpu.VMEM((heads, width), BF16),
            pltpu.VMEM((heads + 2 * slots + GROUP, width), BF16),
            pltpu.VMEM((products, slots, LANES), F32),
            pltpu.VMEM((heads, CHUNK), F32),
            pltpu.VMEM((heads + 2 * slots + GROUP, CHUNK), F32),
        ],
        compiler_params=pltpu.CompilerParams(vmem_limit_bytes=56 * 2**20),
        name="tile",
    )(counts, emb, points, gauss, prompt, mask, sa_qkv, sa_out, t2i, t2i_out, up, down, i2t, i2t_out, hyper, gains)


def seam_call(cov, side, n):
    vmem = pl.BlockSpec(memory_space=pltpu.VMEM)
    return pl.pallas_call(
        functools.partial(seam_kernel, n),
        out_shape=jax.ShapeDtypeStruct((side, side), F32),
        in_specs=[vmem],
        out_specs=vmem,
        scratch_shapes=[
            pltpu.VMEM(cov.shape, F32),
            pltpu.VMEM(cov.shape, F32),
            pltpu.SemaphoreType.DMA((2,)),
            pltpu.SemaphoreType.DMA((2,)),
        ],
        compiler_params=pltpu.CompilerParams(collective_id=0, has_side_effects=True),
        name="seam",
    )(cov)


def shards(
    embedding,
    counts,
    points,
    pe_gauss,
    point_embed,
    mask_token,
    sa_qkv,
    sa_out,
    t2i_qkv,
    t2i_out,
    mlp_up,
    mlp_down,
    i2t_qkv,
    i2t_out,
    hyper_w,
    ln_gains,
):
    side, _, width = embedding.shape
    logits, cov = tile_call(
        counts,
        embedding.reshape(side * side, width),
        points[0, 0],
        pe_gauss,
        point_embed.reshape(1, width),
        mask_token.reshape(1, width),
        sa_qkv,
        sa_out,
        t2i_qkv,
        t2i_out,
        mlp_up,
        mlp_down,
        i2t_qkv,
        i2t_out,
        hyper_w,
        ln_gains,
    )
    blended = seam_call(cov, side, lax.axis_size("col"))
    return logits.reshape(1, 1, *logits.shape), blended


def solution(mesh):
    whole = [P()] * 13
    return jax.shard_map(
        shards,
        mesh=mesh,
        in_specs=(P("row", "col", None), P("col", None), P("row", "col", None, None), *whole),
        out_specs=(P("row", "col", None, None), P("row", "col")),
        check_vma=False,
    )
```

time: 486 us -> 31.4 us (0.06)
  local copies, waits for them, and re-layouts: 208 us -> 1.38 us
  matrix products: 115 us -> 0 us
  other arithmetic: 78.3 us -> 0 us
  waiting for transfers between devices: 35.9 us -> 0 us
  starting transfers between devices: 33.2 us -> 0 us
  Pallas kernels: 8.27 us -> 29.2 us
    gather x80 -> x0, local copies, waits for them, and re-layouts: 146 us -> none  [the longest x32 75.2 us: one_block(): pieces[tile_ids]]
    dot_general x47 -> x0, matrix products: 115 us -> none  [the longest x16 48.4 us: image_side(): jnp.einsum('bpi,id->bpd', mixture, out_weight, preferred_element_type=jnp...]
    reduce_sum x41 -> x0, other arithmetic: 56.9 us -> none  [the longest x16 46.3 us: image_side(): jnp.sum(normed * hyper_rows.astype(jnp.float32)[:, None, :], axis=-1)]
    all_to_all x4 -> x0, waiting for transfers between devices: 32.5 us -> none  [the longest x2 14.4 us: several_exchanges(): lax.all_to_all(slab, axis, split_axis=0, concat_axis=0, tiled=True)]
    pallas_call x0 -> x2, Pallas kernels: none -> 29.2 us  [the longest x1 22.8 us: tile_call(): pl.pallas_call(tile_kernel, out_shape=(jax.ShapeDtypeStruct((slots, cells...]
    while x97 -> x0, local copies, waits for them, and re-layouts: 23.5 us -> none
    all_to_all x4 -> x0, starting transfers between devices: 22.5 us -> none  [the longest x2 13.6 us: several_exchanges(): lax.all_to_all(slab, axis, split_axis=0, concat_axis=0, tiled=True)]
    slice x21 -> x0, local copies, waits for them, and re-layouts: 15 us -> none  [the longest x16 11.1 us: one_block(): ln_gains[3]]
  transfers between devices with their start and end apart: 6 -> 0, of which waited for: 4 -> 0; matrix products, arithmetic and copies ran while one was open for 10% -> 0% of each run, Pallas kernels for 2% -> 0%
where the time goes in v1:
time: 31.4 us; the launch traced here: 31.2 us
  Pallas kernels  29.2 us (93%)
  local copies, waits for them, and re-layouts  1.38 us (4%)
  between operations  0.64 us (2%)
    pallas_call x1, Pallas kernels, tile_call(): pl.pallas_call(tile_kernel, out_shape=(jax.ShapeDtypeStruct((slots, cells...  22.8 us
    pallas_call x1, Pallas kernels, seam_call(): pl.pallas_call(functools.partial(seam_kernel, n), out_shape=jax.ShapeDtyp...  6.37 us
    unnamed x1, local copies, waits for them, and re-layouts  1.38 us

profile of v1, /device:TPU:97, one launch (start us, length us, event | category | flops | bytes accessed | tf_op | source)
XLA Modules:
  0.0 31.2 jit_solution(10066211461580791312)
XLA Ops:
  0.6 22.8 %tile.1 = (bf16[48,4096]{1,0:T(8,128)(2,1)}, f32[32,128]{1,0:T(8,128)}) custom-call(s32[1,16]{1,0:T(1,128)} %counts_ref.1, bf16[4096,256]{1,0:T(8,128)(2,1)} %bitcast.5, s32[2,48]{1,0:T(2,128)} %bitcast.6, f32[2,128]{1,0:T(2,128)} %gauss_ref.1, f32[1,256]{1,0:T(1,128)} %bitcast.7, f32[1,256]{1,0:T(1,128)} %bitcast.8, bf16[256,768]{1,0:T(8,128)(2,1)} %sa_qkv_ref.1, ...), custom_call_target="tpu_custom_call" | custom-call | tf_op jit(solution)/shard_map/tile/pallas_call | solution.py:380
  23.4 6.4 %seam.1 = f32[64,64]{1,0:T(8,128)} custom-call(f32[32,128]{1,0:T(8,128)} %get-tuple-element.5.cov_ref), custom_call_target="tpu_custom_call" | custom-call | tf_op jit(solution)/shard_map/seam/pallas_call | solution.py:410
  29.8 1.4 %copy.19 = f32[64,64]{1,0:T(8,128)} copy(f32[64,64]{1,0:T(8,128)} %seam.1) | data formatting | bytes 32768

commit v2 on v1

v2 whole, which is shorter than its diff:
```python
import functools
import math

import jax
import jax.numpy as jnp
import numpy as np
from jax import lax
from jax.experimental import pallas as pl
from jax.experimental.pallas import tpu as pltpu
from jax.sharding import PartitionSpec as P

HEADS = 8
SEAM = 4
IMG = 1024
EPS = 1e-05
F32 = jnp.float32
BF16 = jnp.bfloat16
LANES = 128
GROUPS = 2
EMB_COPIES = 4
SCORE_CELLS = 1024
LARGE_SUM = 2.0**100
IMAGE_CELLS = 512


def turn_polynomials():
    z = np.linspace(0.0, 0.25, 4001)[1:]
    r = np.sqrt(z)
    fit = np.polynomial.chebyshev.Chebyshev.fit
    power = lambda c: [float(v) for v in c.convert(kind=np.polynomial.Polynomial, domain=[-1, 1]).coef]
    return (
        power(fit(z, np.sin(2 * math.pi * r) / r, 8, domain=[0.0, 0.25])),
        power(fit(z, np.cos(2 * math.pi * r), 8, domain=[0.0, 0.25])),
    )


SIN_COEF, COS_COEF = turn_polynomials()


def sin_cos_turns(turns):
    r = turns - jnp.floor(turns + 0.5)
    z = r * r
    s = jnp.full_like(z, SIN_COEF[-1])
    c = jnp.full_like(z, COS_COEF[-1])
    for a, b in zip(SIN_COEF[-2::-1], COS_COEF[-2::-1]):
        s = s * z + a
        c = c * z + b
    return s * r, c


def dot(a, b):
    return lax.dot_general(a, b, (((1,), (0,)), ((), ())), preferred_element_type=F32)


def dot_t(a, b):
    return lax.dot_general(a, b, (((1,), (1,)), ((), ())), preferred_element_type=F32)


def halves(values):
    high = values.astype(BF16)
    return high, (values - high.astype(F32)).astype(BF16)


def weight_dot(values, weight):
    rows = values.shape[0]
    both = dot(jnp.concatenate(halves(values), axis=0), weight)
    return both[:rows] + both[rows:]


def layer_norm(values, gain):
    centred = values - jnp.mean(values, axis=-1, keepdims=True)
    var = jnp.mean(centred * centred, axis=-1, keepdims=True)
    return centred * lax.rsqrt(var + EPS) * gain


def rounded(values):
    return values.astype(BF16).astype(F32)


def by_head(values):
    lane = lax.broadcasted_iota(jnp.int32, values.shape, 1) // (values.shape[1] // HEADS)
    return jnp.concatenate([jnp.where(lane == h, values, 0.0) for h in range(HEADS)], axis=0)


def centred_rows(values):
    return values - jnp.mean(values, axis=-1, keepdims=True)


def as_column(row):
    n = row.shape[1]
    i = lax.broadcasted_iota(jnp.int32, (n, n), 0)
    j = lax.broadcasted_iota(jnp.int32, (n, n), 1)
    return jnp.sum(jnp.where(i == j, jnp.broadcast_to(row, (n, n)), 0.0), axis=1, keepdims=True)


def tile_kernel(
    counts_ref,
    points_ref,
    gauss_ref,
    prompt_ref,
    mask_ref,
    gains_ref,
    emb_hbm,
    sa_qkv_hbm,
    sa_out_hbm,
    t2i_hbm,
    t2i_out_hbm,
    up_hbm,
    down_hbm,
    i2t_hbm,
    i2t_out_hbm,
    hyper_hbm,
    logits_hbm,
    cov_ref,
    emb_ref,
    sa_qkv_ref,
    sa_out_ref,
    t2i_ref,
    t2i_out_ref,
    up_ref,
    down_ref,
    i2t_ref,
    i2t_out_ref,
    hyper_ref,
    logits_ref,
    keys_ref,
    sq_ref,
    prob_ref,
    aq_ref,
    top_ref,
    sum_ref,
    start_ref,
    queries_ref,
    cross_ref,
    back_ref,
    hyper_out,
    gap_ref,
    row_ref,
    mix_ref,
    t_ref,
    table_ref,
    in_sem,
    emb_sem,
    out_sem,
):
    cells, width = emb_ref.shape
    slots = points_ref.shape[1]
    tokens = 2 * slots
    half = width // 2
    inner = t2i_ref.shape[1] // 3
    side = math.isqrt(cells)
    count = counts_ref[0, lax.axis_index("row")]

    weights = [
        pltpu.make_async_copy(source, target, in_sem.at[i])
        for i, (source, target) in enumerate(
            [
                (sa_qkv_hbm, sa_qkv_ref),
                (sa_out_hbm, sa_out_ref),
                (t2i_hbm, t2i_ref),
                (t2i_out_hbm, t2i_out_ref),
                (up_hbm, up_ref),
                (down_hbm, down_ref),
                (i2t_hbm, i2t_ref),
                (hyper_hbm, hyper_ref),
                (i2t_out_hbm, i2t_out_ref),
            ]
        )
    ]
    step = cells // EMB_COPIES
    cell_copies = [
        pltpu.make_async_copy(emb_hbm.at[pl.ds(i * step, step)], emb_ref.at[pl.ds(i * step, step)], emb_sem.at[i])
        for i in range(EMB_COPIES)
    ]
    for copy in weights[:3] + cell_copies + weights[3:]:
        copy.start()

    steps = (2.0 * (lax.broadcasted_iota(jnp.int32, (side, half), 0).astype(F32) + 0.5)) / side - 1.0
    sin_x, cos_x = sin_cos_turns(steps * gauss_ref[0:1, :])
    sin_y, cos_y = sin_cos_turns(steps * gauss_ref[1:2, :])

    coords = (2.0 * (points_ref[...].astype(F32) + 0.5)) / IMG - 1.0
    turns = as_column(coords[0:1, :]) * gauss_ref[0:1, :] + as_column(coords[1:2, :]) * gauss_ref[1:2, :]
    sin_p, cos_p = sin_cos_turns(turns)
    prompt = jnp.concatenate([sin_p, cos_p], axis=1) + prompt_ref[...]
    start = jnp.concatenate([jnp.broadcast_to(mask_ref[...], (slots, width)), prompt], axis=0)
    weights[0].wait()
    qkv = weight_dot(start, sa_qkv_ref[...])
    q, k, v = qkv[:, :width], qkv[:, width : 2 * width], qkv[:, 2 * width :]
    k_gap = k[slots:] - k[:slots]
    v_gap = v[slots:] - v[:slots]
    self_width = width // HEADS
    i = lax.broadcasted_iota(jnp.int32, (width, width), 0) // self_width
    j = lax.broadcasted_iota(jnp.int32, (width, width), 1) // self_width
    same = jnp.where(i == j, 1.0, 0.0).astype(BF16)
    gap = weight_dot(q * jnp.concatenate([k_gap, k_gap], axis=0), same) / math.sqrt(self_width)
    second = jax.nn.sigmoid(gap)
    joined = jnp.concatenate([v[:slots], v[:slots]], axis=0) + second * jnp.concatenate([v_gap, v_gap], axis=0)
    weights[1].wait()
    queries = layer_norm(weight_dot(joined, sa_out_ref[...]), gains_ref[0:1, :])
    weights[2].wait()
    cross_q = rounded(weight_dot(queries + start, t2i_ref[:, :inner]))
    scale = math.log2(math.e) / math.sqrt(inner // HEADS)
    aq_ref[...] = (dot_t(by_head(cross_q).astype(BF16), t2i_ref[:, inner : 2 * inner]) * scale).astype(BF16)

    table_ref[0] = sin_y
    table_ref[1] = cos_y
    start_ref[...] = start
    queries_ref[...] = queries

    for y in range(side):
        if y * side % step == 0:
            cell_copies[y * side // step].wait()
        rows = slice(y * side, (y + 1) * side)
        e = emb_ref[rows, :].astype(F32)
        sy, cy = table_ref[0, y : y + 1, :], table_ref[1, y : y + 1, :]
        e1, e2 = e[:, :half], e[:, half:]
        keys_ref[rows, :half] = (e1 + (sin_x * cy + cos_x * sy)).astype(BF16)
        keys_ref[rows, half:] = (e2 + (cos_x * cy - sin_x * sy)).astype(BF16)
        high, low = halves(e1 * e1 + e2 * e2)
        sq_ref[rows, :half] = high
        sq_ref[rows, half:] = low

    pairs = HEADS * tokens

    def scores(at):
        return dot_t(aq_ref[...], keys_ref[pl.ds(at, SCORE_CELLS), :])

    def probabilities(at, s):
        for r0 in range(0, pairs, 16):
            rows = slice(r0, r0 + 16)
            top = top_ref[rows, :]
            total = sum_ref[rows, :]
            for k0 in range(0, SCORE_CELLS, LANES):
                p = jnp.exp2(s[rows, k0 : k0 + LANES] - top)
                total = total + p
                prob_ref[rows, pl.ds(pl.multiple_of(at + k0, LANES), LANES)] = p.astype(BF16)
            sum_ref[rows, :] = total

    def prob_step(c, carry):
        at = pl.multiple_of(c * SCORE_CELLS, SCORE_CELLS)
        probabilities(at, scores(at))
        return carry

    sum_ref[...] = jnp.zeros_like(sum_ref)
    first = scores(0)
    top_ref[...] = jnp.broadcast_to(jnp.max(first, axis=1, keepdims=True), top_ref.shape)
    probabilities(0, first)
    lax.fori_loop(1, cells // SCORE_CELLS, prob_step, 0)

    @pl.when(jnp.logical_not(jnp.max(sum_ref[...]) < LARGE_SUM))
    def _():
        top_ref[...] = jnp.full(top_ref.shape, -jnp.inf, F32)

        def top_step(c, carry):
            s = scores(pl.multiple_of(c * SCORE_CELLS, SCORE_CELLS))
            for k0 in range(0, SCORE_CELLS, LANES):
                top_ref[...] = jnp.maximum(top_ref[...], s[:, k0 : k0 + LANES])
            return carry

        lax.fori_loop(0, cells // SCORE_CELLS, top_step, 0)
        top_ref[...] = jnp.broadcast_to(jnp.max(top_ref[...], axis=1, keepdims=True), top_ref.shape)
        sum_ref[...] = jnp.zeros_like(sum_ref)
        lax.fori_loop(0, cells // SCORE_CELLS, prob_step, 0)

    @pl.when(count > 0)
    def _():
        mean_cell = dot(prob_ref[...], emb_ref[...]) / jnp.sum(sum_ref[...], axis=1, keepdims=True)
        head_out = dot(mean_cell.astype(BF16), t2i_ref[:, 2 * inner :])
        lane = lax.broadcasted_iota(jnp.int32, (tokens, inner), 1) // (inner // HEADS)
        cross_out = jnp.zeros((tokens, inner), F32)
        for h in range(HEADS):
            cross_out = jnp.where(lane == h, head_out[h * tokens : (h + 1) * tokens], cross_out)
        cross_ref[...] = cross_out

    @pl.when(count > 0)
    def _():
        for copy in weights[3:]:
            copy.wait()
        queries = layer_norm(queries_ref[...] + weight_dot(cross_ref[...], t2i_out_ref[...]), gains_ref[1:2, :])
        hidden = jnp.maximum(weight_dot(queries, up_ref[...]), 0.0)
        queries = layer_norm(queries + weight_dot(hidden, down_ref[...]), gains_ref[2:3, :])
        start = start_ref[...]
        back_k = rounded(weight_dot(queries + start, i2t_ref[:, inner : 2 * inner]))
        back_v = rounded(weight_dot(queries, i2t_ref[:, 2 * inner :]))
        hyper = rounded(weight_dot(jnp.maximum(weight_dot(queries[:slots], hyper_ref[0]), 0.0), hyper_ref[1]))
        back_ref[0] = back_k
        back_ref[1] = back_v
        hyper_out[...] = hyper

    group = slots // GROUPS
    heads = HEADS * group
    lines = heads + 2 * group
    blank = width - heads

    @pl.when(count > 0)
    def _():
        back_k, back_v, hyper = back_ref[0], back_ref[1], hyper_out[...]
        key_gap = back_k[:slots] - back_k[slots:]
        gap_scale = 0.5 / math.sqrt(inner // HEADS)
        spread = 0.5 * (back_v[:slots] - back_v[slots:])
        middle = 0.5 * (back_v[:slots] + back_v[slots:])
        b_all = rounded(centred_rows(weight_dot(middle, i2t_out_ref[...])))
        g_all = rounded(centred_rows(hyper * gains_ref[3:4, :]))
        zeros = jnp.zeros((blank, width), BF16)
        r = lax.broadcasted_iota(jnp.int32, (lines, width), 0)
        c = lax.broadcasted_iota(jnp.int32, (lines, width), 1)
        own_slot = jnp.logical_and(r % group == c % group, c < heads)
        for n in range(GROUPS):
            of = slice(n * group, (n + 1) * group)
            gap_ref[n * heads : (n + 1) * heads, :] = (
                dot_t(by_head(key_gap[of]).astype(BF16), i2t_ref[:, :inner]) * gap_scale
            ).astype(BF16)
            u = rounded(centred_rows(dot(by_head(spread[of]).astype(BF16), i2t_out_ref[...])))
            b, g = b_all[of], g_all[of]
            left = jnp.concatenate([u, 2.0 * b, g], axis=0).astype(BF16)
            right = jnp.concatenate([u.astype(BF16), zeros], axis=0)
            constant = jnp.concatenate(
                [
                    jnp.zeros((heads, 1), F32),
                    jnp.sum(b * b, axis=1, keepdims=True),
                    jnp.sum(b * g, axis=1, keepdims=True),
                ],
                axis=0,
            )
            high = rounded(constant)
            mix = jnp.where(own_slot, dot_t(left, right), 0.0)
            mix = jnp.where(c == heads, high, jnp.where(c == heads + 1, constant - high, mix))
            mix_ref[n] = mix.astype(BF16)
            row_ref[n * lines : (n + 1) * lines, :] = jnp.concatenate([2.0 * u, 2.0 * b, g], axis=0).astype(BF16)

    ones = jnp.ones((16, width), BF16)
    row_ref[GROUPS * lines :, :] = ones
    t_ref[:, heads:, :] = jnp.ones((GROUPS, blank, cells), BF16)

    out_copies = []
    for at in range(0, cells, IMAGE_CELLS):
        here = slice(at, at + IMAGE_CELLS)
        t = jnp.tanh(dot_t(gap_ref[...], keys_ref[here, :])).astype(BF16)
        for n in range(GROUPS):
            t_ref[n, :heads, here] = t[n * heads : (n + 1) * heads]
        cell_part = dot_t(row_ref[...], emb_ref[here, :])
        sums = cell_part[GROUPS * lines : GROUPS * lines + 8]
        own = dot_t(ones, sq_ref[here, :])[:8] - sums * sums * (1.0 / width)
        logits = []
        for n in range(GROUPS):
            line = cell_part[n * lines : (n + 1) * lines] + dot(mix_ref[n], t_ref[n, :, here])
            t32 = t[n * heads : (n + 1) * heads].astype(F32)
            var = line[heads : heads + group] + jnp.concatenate([own] * (group // 8), axis=0)
            for h in range(HEADS):
                var = var + t32[h * group : (h + 1) * group] * line[h * group : (h + 1) * group]
            var = jnp.maximum(var, 0.0)
            logits.append(line[heads + group :] * lax.rsqrt(var + EPS * width))
        logit = rounded(jnp.concatenate(logits, axis=0))
        live = lax.broadcasted_iota(jnp.int32, logit.shape, 0) < count
        masked = jnp.where(live, logit, 0.0)
        logits_ref[:, here] = masked.astype(BF16)
        out_copies.append(pltpu.make_async_copy(logits_ref.at[:, here], logits_hbm.at[:, here], out_sem.at[at // IMAGE_CELLS]))
        out_copies[-1].start()
        cover = jnp.sum(jnp.where(live, jax.nn.sigmoid(masked), 0.0), axis=0, keepdims=True)
        for k0 in range(0, IMAGE_CELLS, LANES):
            cov_ref[(at + k0) // LANES : (at + k0) // LANES + 1, :] = cover[:, k0 : k0 + LANES]
    for copy in out_copies:
        copy.wait()


def seam_kernel(n, cov_ref, out_ref, left_ref, right_ref, send_sem, recv_sem):
    me = lax.axis_index("col")
    side = out_ref.shape[0]
    has_left, has_right = me > 0, me < n - 1
    barrier = pltpu.get_barrier_semaphore()
    mesh_id = pl.DeviceIdType.MESH

    def to_left():
        return pltpu.make_async_remote_copy(
            src_ref=cov_ref,
            dst_ref=right_ref,
            send_sem=send_sem.at[0],
            recv_sem=recv_sem.at[0],
            device_id={"col": me - 1},
            device_id_type=mesh_id,
        )

    def to_right():
        return pltpu.make_async_remote_copy(
            src_ref=cov_ref,
            dst_ref=left_ref,
            send_sem=send_sem.at[1],
            recv_sem=recv_sem.at[1],
            device_id={"col": me + 1},
            device_id_type=mesh_id,
        )

    @pl.when(has_left)
    def _():
        pl.semaphore_signal(barrier, inc=1, device_id={"col": me - 1}, device_id_type=mesh_id)

    @pl.when(has_right)
    def _():
        pl.semaphore_signal(barrier, inc=1, device_id={"col": me + 1}, device_id_type=mesh_id)

    pl.semaphore_wait(barrier, has_left.astype(jnp.int32) + has_right.astype(jnp.int32))

    @pl.when(has_left)
    def _():
        to_left().start()

    @pl.when(has_right)
    def _():
        to_right().start()

    cov = cov_ref[...]
    x = lax.broadcasted_iota(jnp.int32, cov.shape, 1) % side
    total = (SEAM + 1.0) * cov
    for d in range(1, SEAM + 1):
        inside = jnp.where(x < side - d, pltpu.roll(cov, LANES - d, 1), 0.0)
        inside = inside + jnp.where(x >= d, pltpu.roll(cov, d, 1), 0.0)
        total = total + (SEAM + 1.0 - d) * inside

    @pl.when(jnp.logical_not(has_left))
    def _():
        left_ref[...] = jnp.zeros_like(left_ref)

    @pl.when(jnp.logical_not(has_right))
    def _():
        right_ref[...] = jnp.zeros_like(right_ref)

    @pl.when(has_right)
    def _():
        to_right().wait_send()
        to_left().wait_recv()

    @pl.when(has_left)
    def _():
        to_left().wait_send()
        to_right().wait_recv()

    left, right = left_ref[...], right_ref[...]
    for d in range(1, SEAM + 1):
        outside = jnp.where(x >= side - d, pltpu.roll(right, side - d, 1), 0.0)
        outside = outside + jnp.where(x < d, pltpu.roll(left, side + d, 1), 0.0)
        total = total + (SEAM + 1.0 - d) * outside
    total = total * (1.0 / (SEAM + 1) ** 2)
    out_ref[pl.ds(0, side // 2, stride=2), :] = total[:, :side]
    out_ref[pl.ds(1, side // 2, stride=2), :] = total[:, side:]


def tile_call(counts, emb, points, gauss, prompt, mask, sa_qkv, sa_out, t2i, t2i_out, up, down, i2t, i2t_out, hyper, gains):
    cells, width = emb.shape
    slots = points.shape[1]
    rows = 2 * slots * HEADS
    heads = HEADS * slots // GROUPS
    lines = heads + 2 * slots // GROUPS
    vmem = pl.BlockSpec(memory_space=pltpu.VMEM)
    hbm = pl.BlockSpec(memory_space=pl.ANY)
    large = [emb, sa_qkv, sa_out, t2i, t2i_out, up, down, i2t, i2t_out, hyper]
    return pl.pallas_call(
        tile_kernel,
        out_shape=(
            jax.ShapeDtypeStruct((slots, cells), BF16),
            jax.ShapeDtypeStruct((cells // LANES, LANES), F32),
        ),
        in_specs=[pl.BlockSpec(memory_space=pltpu.SMEM)] + [vmem] * 5 + [hbm] * len(large),
        out_specs=(hbm, vmem),
        scratch_shapes=[pltpu.VMEM(a.shape, a.dtype) for a in large]
        + [
            pltpu.VMEM((slots, cells), BF16),
            pltpu.VMEM((cells, width), BF16),
            pltpu.VMEM((cells, width), BF16),
            pltpu.VMEM((rows, cells), BF16),
            pltpu.VMEM((rows, width), BF16),
            pltpu.VMEM((rows, LANES), F32),
            pltpu.VMEM((rows, LANES), F32),
            pltpu.VMEM((2 * slots, width), F32),
            pltpu.VMEM((2 * slots, width), F32),
            pltpu.VMEM((2 * slots, t2i.shape[1] // 3), F32),
            pltpu.VMEM((2, 2 * slots, t2i.shape[1] // 3), F32),
            pltpu.VMEM((slots, width), F32),
            pltpu.VMEM((GROUPS * heads, width), BF16),
            pltpu.VMEM((GROUPS * lines + 16, width), BF16),
            pltpu.VMEM((GROUPS, lines, width), BF16),
            pltpu.VMEM((GROUPS, width, cells), BF16),
            pltpu.VMEM((2, math.isqrt(cells), width // 2), F32),
            pltpu.SemaphoreType.DMA((len(large) - 1,)),
            pltpu.SemaphoreType.DMA((EMB_COPIES,)),
            pltpu.SemaphoreType.DMA((cells // IMAGE_CELLS,)),
        ],
        compiler_params=pltpu.CompilerParams(vmem_limit_bytes=58 * 2**20),
        name="tile",
    )(counts, points, gauss, prompt, mask, gains, *large)


def seam_call(cov, side, n):
    vmem = pl.BlockSpec(memory_space=pltpu.VMEM)
    return pl.pallas_call(
        functools.partial(seam_kernel, n),
        out_shape=jax.ShapeDtypeStruct((side, side), F32),
        in_specs=[vmem],
        out_specs=vmem,
        scratch_shapes=[
            pltpu.VMEM(cov.shape, F32),
            pltpu.VMEM(cov.shape, F32),
            pltpu.SemaphoreType.DMA((2,)),
            pltpu.SemaphoreType.DMA((2,)),
        ],
        compiler_params=pltpu.CompilerParams(collective_id=0, has_side_effects=True),
        name="seam",
    )(cov)


def shards(
    embedding,
    counts,
    points,
    pe_gauss,
    point_embed,
    mask_token,
    sa_qkv,
    sa_out,
    t2i_qkv,
    t2i_out,
    mlp_up,
    mlp_down,
    i2t_qkv,
    i2t_out,
    hyper_w,
    ln_gains,
):
    side, _, width = embedding.shape
    logits, cov = tile_call(
        counts,
        embedding.reshape(side * side, width),
        points[0, 0],
        pe_gauss,
        point_embed.reshape(1, width),
        mask_token.reshape(1, width),
        sa_qkv,
        sa_out,
        t2i_qkv,
        t2i_out,
        mlp_up,
        mlp_down,
        i2t_qkv,
        i2t_out,
        hyper_w,
        ln_gains,
    )
    blended = seam_call(cov, side, lax.axis_size("col"))
    return logits.reshape(1, 1, *logits.shape), blended


def solution(mesh):
    whole = [P()] * 13
    return jax.shard_map(
        shards,
        mesh=mesh,
        in_specs=(P("row", "col", None), P("col", None), P("row", "col", None, None), *whole),
        out_specs=(P("row", "col", None, None), P("row", "col")),
        check_vma=False,
    )
```

time: 31.4 us -> 26.7 us (0.85)
  Pallas kernels: 29.2 us -> 24.5 us
    pallas_call x1, Pallas kernels: 22.8 us -> 17.9 us  [tile_call(): pl.pallas_call(tile_kernel, out_shape=(jax.ShapeDtypeStruct((slots, cells...]
where the time goes in v2:
time: 26.7 us; the launch traced here: 26.5 us
  Pallas kernels  24.5 us (92%)
  local copies, waits for them, and re-layouts  1.38 us (5%)
  between operations  0.65 us (2%)
    pallas_call x1, Pallas kernels, tile_call(): pl.pallas_call(tile_kernel, out_shape=(jax.ShapeDtypeStruct((slots, cells...  17.9 us
    pallas_call x1, Pallas kernels, seam_call(): pl.pallas_call(functools.partial(seam_kernel, n), out_shape=jax.ShapeDtyp...  6.52 us
    unnamed x1, local copies, waits for them, and re-layouts  1.38 us

profile of v2, /device:TPU:97, one launch (start us, length us, event | category | flops | bytes accessed | tf_op | source)
XLA Modules:
  0.0 26.5 jit_solution(2239951820579489218)
XLA Ops:
  0.6 17.9 %tile.1 = (bf16[48,4096]{1,0:T(8,128)(2,1)}, f32[32,128]{1,0:T(8,128)}) custom-call(s32[1,16]{1,0:T(1,128)} %counts_ref.1, s32[2,48]{1,0:T(2,128)} %bitcast.6, f32[2,128]{1,0:T(2,128)} %gauss_ref.1, f32[1,256]{1,0:T(1,128)} %bitcast.7, f32[1,256]{1,0:T(1,128)} %bitcast.8, f32[4,256]{1,0:T(4,128)} %gains_ref.1, bf16[4096,256]{1,0:T(8,128)(2,1)} %bitcast.5, ...), custom_call_target="tpu_custom_call" | custom-call | tf_op jit(solution)/shard_map/tile/pallas_call | solution.py:457
  18.6 6.5 %seam.1 = f32[64,64]{1,0:T(8,128)} custom-call(f32[32,128]{1,0:T(8,128)} %get-tuple-element.5.cov_ref), custom_call_target="tpu_custom_call" | custom-call | tf_op jit(solution)/shard_map/seam/pallas_call | solution.py:495
  25.1 1.4 %copy.19 = f32[64,64]{1,0:T(8,128)} copy(f32[64,64]{1,0:T(8,128)} %seam.1) | data formatting | bytes 32768

commit v3 on v2

--- a/solution.py
+++ b/solution.py
@@ -124,7 +124,6 @@
     hyper_ref,
     logits_ref,
     keys_ref,
-    sq_ref,
     prob_ref,
     aq_ref,
     top_ref,
@@ -217,9 +216,6 @@
         e1, e2 = e[:, :half], e[:, half:]
         keys_ref[rows, :half] = (e1 + (sin_x * cy + cos_x * sy)).astype(BF16)
         keys_ref[rows, half:] = (e2 + (cos_x * cy - sin_x * sy)).astype(BF16)
-        high, low = halves(e1 * e1 + e2 * e2)
-        sq_ref[rows, :half] = high
-        sq_ref[rows, half:] = low
 
     pairs = HEADS * tokens
 
@@ -278,8 +274,8 @@
         for copy in weights[3:]:
             copy.wait()
         queries = layer_norm(queries_ref[...] + weight_dot(cross_ref[...], t2i_out_ref[...]), gains_ref[1:2, :])
-        hidden = jnp.maximum(weight_dot(queries, up_ref[...]), 0.0)
-        queries = layer_norm(queries + weight_dot(hidden, down_ref[...]), gains_ref[2:3, :])
+        hidden = jnp.maximum(dot(queries.astype(BF16), up_ref[...]), 0.0)
+        queries = layer_norm(queries + dot(hidden.astype(BF16), down_ref[...]), gains_ref[2:3, :])
         start = start_ref[...]
         back_k = rounded(weight_dot(queries + start, i2t_ref[:, inner : 2 * inner]))
         back_v = rounded(weight_dot(queries, i2t_ref[:, 2 * inner :]))
@@ -341,7 +337,9 @@
             t_ref[n, :heads, here] = t[n * heads : (n + 1) * heads]
         cell_part = dot_t(row_ref[...], emb_ref[here, :])
         sums = cell_part[GROUPS * lines : GROUPS * lines + 8]
-        own = dot_t(ones, sq_ref[here, :])[:8] - sums * sums * (1.0 / width)
+        e = emb_ref[here, :].astype(F32)
+        squares = jnp.concatenate(halves(e[:, :half] * e[:, :half] + e[:, half:] * e[:, half:]), axis=1)
+        own = dot_t(ones, squares)[:8] - sums * sums * (1.0 / width)
         logits = []
         for n in range(GROUPS):
             line = cell_part[n * lines : (n + 1) * lines] + dot(mix_ref[n], t_ref[n, :, here])
@@ -364,16 +362,18 @@
         copy.wait()
 
 
-def seam_kernel(n, cov_ref, out_ref, left_ref, right_ref, send_sem, recv_sem):
+def seam_kernel(n, cov_hbm, out_ref, cov_ref, left_ref, right_ref, send_sem, recv_sem, own_sem):
     me = lax.axis_index("col")
     side = out_ref.shape[0]
     has_left, has_right = me > 0, me < n - 1
     barrier = pltpu.get_barrier_semaphore()
     mesh_id = pl.DeviceIdType.MESH
+    own_copy = pltpu.make_async_copy(cov_hbm, cov_ref, own_sem)
+    own_copy.start()
 
     def to_left():
         return pltpu.make_async_remote_copy(
-            src_ref=cov_ref,
+            src_ref=cov_hbm,
             dst_ref=right_ref,
             send_sem=send_sem.at[0],
             recv_sem=recv_sem.at[0],
@@ -383,7 +383,7 @@
 
     def to_right():
         return pltpu.make_async_remote_copy(
-            src_ref=cov_ref,
+            src_ref=cov_hbm,
             dst_ref=left_ref,
             send_sem=send_sem.at[1],
             recv_sem=recv_sem.at[1],
@@ -409,6 +409,7 @@
     def _():
         to_right().start()
 
+    own_copy.wait()
     cov = cov_ref[...]
     x = lax.broadcasted_iota(jnp.int32, cov.shape, 1) % side
     total = (SEAM + 1.0) * cov
@@ -465,7 +466,6 @@
         scratch_shapes=[pltpu.VMEM(a.shape, a.dtype) for a in large]
         + [
             pltpu.VMEM((slots, cells), BF16),
-            pltpu.VMEM((cells, width), BF16),
             pltpu.VMEM((cells, width), BF16),
             pltpu.VMEM((rows, cells), BF16),
             pltpu.VMEM((rows, width), BF16),
@@ -495,13 +495,15 @@
     return pl.pallas_call(
         functools.partial(seam_kernel, n),
         out_shape=jax.ShapeDtypeStruct((side, side), F32),
-        in_specs=[vmem],
+        in_specs=[pl.BlockSpec(memory_space=pl.ANY)],
         out_specs=vmem,
         scratch_shapes=[
             pltpu.VMEM(cov.shape, F32),
             pltpu.VMEM(cov.shape, F32),
+            pltpu.VMEM(cov.shape, F32),
             pltpu.SemaphoreType.DMA((2,)),
             pltpu.SemaphoreType.DMA((2,)),
+            pltpu.SemaphoreType.DMA(()),
         ],
         compiler_params=pltpu.CompilerParams(collective_id=0, has_side_effects=True),
         name="seam",

time: 26.7 us -> 25.3 us (0.948)
  Pallas kernels: 24.5 us -> 23.1 us
    pallas_call x1, Pallas kernels: 17.9 us -> 17 us  [tile_call(): pl.pallas_call(tile_kernel, out_shape=(jax.ShapeDtypeStruct((slots, cells...]
    pallas_call x1, Pallas kernels: 6.52 us -> 6.09 us  [seam_call(): pl.pallas_call(functools.partial(seam_kernel, n), out_shape=jax.ShapeDtyp...]
where the time goes in v3:
time: 25.3 us; the launch traced here: 25.1 us
  Pallas kernels  23.1 us (91%)
  local copies, waits for them, and re-layouts  1.38 us (5%)
  between operations  0.65 us (3%)
    pallas_call x1, Pallas kernels, tile_call(): pl.pallas_call(tile_kernel, out_shape=(jax.ShapeDtypeStruct((slots, cells...  17 us
    pallas_call x1, Pallas kernels, seam_call(): pl.pallas_call(functools.partial(seam_kernel, n), out_shape=jax.ShapeDtyp...  6.09 us
    unnamed x1, local copies, waits for them, and re-layouts  1.38 us

profile of v3, /device:TPU:97, one launch (start us, length us, event | category | flops | bytes accessed | tf_op | source)
XLA Modules:
  0.0 25.1 jit_solution(5883911360191815283)
XLA Ops:
  0.6 17.0 %tile.1 = (bf16[48,4096]{1,0:T(8,128)(2,1)}, f32[32,128]{1,0:T(8,128)}) custom-call(s32[1,16]{1,0:T(1,128)} %counts_ref.1, s32[2,48]{1,0:T(2,128)} %bitcast.6, f32[2,128]{1,0:T(2,128)} %gauss_ref.1, f32[1,256]{1,0:T(1,128)} %bitcast.7, f32[1,256]{1,0:T(1,128)} %bitcast.8, f32[4,256]{1,0:T(4,128)} %gains_ref.1, bf16[4096,256]{1,0:T(8,128)(2,1)} %bitcast.5, ...), custom_call_target="tpu_custom_call" | custom-call | tf_op jit(solution)/shard_map/tile/pallas_call | solution.py:458
  17.6 6.1 %seam.1 = f32[64,64]{1,0:T(8,128)} custom-call(f32[32,128]{1,0:T(8,128)} %get-tuple-element.5.cov_hbm), custom_call_target="tpu_custom_call" | custom-call | tf_op jit(solution)/shard_map/seam/pallas_call | solution.py:495
  23.7 1.4 %copy.19 = f32[64,64]{1,0:T(8,128)} copy(f32[64,64]{1,0:T(8,128)} %seam.1) | data formatting | bytes 32768

commit v4 on v3

--- a/solution.py
+++ b/solution.py
@@ -112,6 +112,7 @@
     hyper_hbm,
     logits_hbm,
     cov_ref,
+    tail_ref,
     emb_ref,
     sa_qkv_ref,
     sa_out_ref,
@@ -356,25 +357,24 @@
         out_copies.append(pltpu.make_async_copy(logits_ref.at[:, here], logits_hbm.at[:, here], out_sem.at[at // IMAGE_CELLS]))
         out_copies[-1].start()
         cover = jnp.sum(jnp.where(live, jax.nn.sigmoid(masked), 0.0), axis=0, keepdims=True)
-        for k0 in range(0, IMAGE_CELLS, LANES):
-            cov_ref[(at + k0) // LANES : (at + k0) // LANES + 1, :] = cover[:, k0 : k0 + LANES]
+        for k0 in range(0, IMAGE_CELLS, side):
+            cov_ref[(at + k0) // side : (at + k0) // side + 1, :] = cover[:, k0 : k0 + side]
+    cov = cov_ref[...]
+    tail_ref[...] = jnp.concatenate([cov[:, side - SEAM :], cov[:, : side - SEAM]], axis=1)
     for copy in out_copies:
         copy.wait()
 
 
-def seam_kernel(n, cov_hbm, out_ref, cov_ref, left_ref, right_ref, send_sem, recv_sem, own_sem):
+def seam_kernel(n, cov_hbm, tail_hbm, left_hbm, right_hbm, zero_ref, send_sem, recv_sem, zero_sem):
     me = lax.axis_index("col")
-    side = out_ref.shape[0]
     has_left, has_right = me > 0, me < n - 1
     barrier = pltpu.get_barrier_semaphore()
     mesh_id = pl.DeviceIdType.MESH
-    own_copy = pltpu.make_async_copy(cov_hbm, cov_ref, own_sem)
-    own_copy.start()
 
     def to_left():
         return pltpu.make_async_remote_copy(
             src_ref=cov_hbm,
-            dst_ref=right_ref,
+            dst_ref=right_hbm,
             send_sem=send_sem.at[0],
             recv_sem=recv_sem.at[0],
             device_id={"col": me - 1},
@@ -383,8 +383,8 @@
 
     def to_right():
         return pltpu.make_async_remote_copy(
-            src_ref=cov_hbm,
-            dst_ref=left_ref,
+            src_ref=tail_hbm,
+            dst_ref=left_hbm,
             send_sem=send_sem.at[1],
             recv_sem=recv_sem.at[1],
             device_id={"col": me + 1},
@@ -409,22 +409,19 @@
     def _():
         to_right().start()
 
-    own_copy.wait()
-    cov = cov_ref[...]
-    x = lax.broadcasted_iota(jnp.int32, cov.shape, 1) % side
-    total = (SEAM + 1.0) * cov
-    for d in range(1, SEAM + 1):
-        inside = jnp.where(x < side - d, pltpu.roll(cov, LANES - d, 1), 0.0)
-        inside = inside + jnp.where(x >= d, pltpu.roll(cov, d, 1), 0.0)
-        total = total + (SEAM + 1.0 - d) * inside
-
     @pl.when(jnp.logical_not(has_left))
     def _():
-        left_ref[...] = jnp.zeros_like(left_ref)
+        zero_ref[...] = jnp.zeros_like(zero_ref)
+        copy = pltpu.make_async_copy(zero_ref, left_hbm, zero_sem)
+        copy.start()
+        copy.wait()
 
     @pl.when(jnp.logical_not(has_right))
     def _():
-        right_ref[...] = jnp.zeros_like(right_ref)
+        zero_ref[...] = jnp.zeros_like(zero_ref)
+        copy = pltpu.make_async_copy(zero_ref, right_hbm, zero_sem)
+        copy.start()
+        copy.wait()
 
     @pl.when(has_right)
     def _():
@@ -435,15 +432,6 @@
     def _():
         to_left().wait_send()
         to_right().wait_recv()
-
-    left, right = left_ref[...], right_ref[...]
-    for d in range(1, SEAM + 1):
-        outside = jnp.where(x >= side - d, pltpu.roll(right, side - d, 1), 0.0)
-        outside = outside + jnp.where(x < d, pltpu.roll(left, side + d, 1), 0.0)
-        total = total + (SEAM + 1.0 - d) * outside
-    total = total * (1.0 / (SEAM + 1) ** 2)
-    out_ref[pl.ds(0, side // 2, stride=2), :] = total[:, :side]
-    out_ref[pl.ds(1, side // 2, stride=2), :] = total[:, side:]
 
 
 def tile_call(counts, emb, points, gauss, prompt, mask, sa_qkv, sa_out, t2i, t2i_out, up, down, i2t, i2t_out, hyper, gains):
@@ -459,10 +447,11 @@
         tile_kernel,
         out_shape=(
             jax.ShapeDtypeStruct((slots, cells), BF16),
-            jax.ShapeDtypeStruct((cells // LANES, LANES), F32),
+            jax.ShapeDtypeStruct((math.isqrt(cells),) * 2, F32),
+            jax.ShapeDtypeStruct((math.isqrt(cells),) * 2, F32),
         ),
         in_specs=[pl.BlockSpec(memory_space=pltpu.SMEM)] + [vmem] * 5 + [hbm] * len(large),
-        out_specs=(hbm, vmem),
+        out_specs=(hbm, vmem, vmem),
         scratch_shapes=[pltpu.VMEM(a.shape, a.dtype) for a in large]
         + [
             pltpu.VMEM((slots, cells), BF16),
@@ -490,16 +479,14 @@
     )(counts, points, gauss, prompt, mask, gains, *large)
 
 
-def seam_call(cov, side, n):
-    vmem = pl.BlockSpec(memory_space=pltpu.VMEM)
+def seam_call(cov, tail, n):
+    hbm = pl.BlockSpec(memory_space=pl.ANY)
     return pl.pallas_call(
         functools.partial(seam_kernel, n),
-        out_shape=jax.ShapeDtypeStruct((side, side), F32),
-        in_specs=[pl.BlockSpec(memory_space=pl.ANY)],
-        out_specs=vmem,
+        out_shape=(jax.ShapeDtypeStruct(cov.shape, F32), jax.ShapeDtypeStruct(cov.shape, F32)),
+        in_specs=[hbm, hbm],
+        out_specs=(hbm, hbm),
         scratch_shapes=[
-            pltpu.VMEM(cov.shape, F32),
-            pltpu.VMEM(cov.shape, F32),
             pltpu.VMEM(cov.shape, F32),
             pltpu.SemaphoreType.DMA((2,)),
             pltpu.SemaphoreType.DMA((2,)),
@@ -507,7 +494,17 @@
         ],
         compiler_params=pltpu.CompilerParams(collective_id=0, has_side_effects=True),
         name="seam",
-    )(cov)
+    )(cov, tail)
+
+
+def blend(left, cov, right):
+    side = cov.shape[1]
+    padded = jnp.concatenate([left[:, :SEAM], cov, right[:, :SEAM]], axis=1)
+    blended = jnp.zeros_like(cov)
+    for offset in range(-SEAM, SEAM + 1):
+        factor = (SEAM + 1 - abs(offset)) / (SEAM + 1) ** 2
+        blended = blended + factor * padded[:, SEAM + offset : SEAM + offset + side]
+    return blended
 
 
 def shards(
@@ -529,7 +526,7 @@
     ln_gains,
 ):
     side, _, width = embedding.shape
-    logits, cov = tile_call(
+    logits, cov, tail = tile_call(
         counts,
         embedding.reshape(side * side, width),
         points[0, 0],
@@ -547,7 +544,8 @@
         hyper_w,
         ln_gains,
     )
-    blended = seam_call(cov, side, lax.axis_size("col"))
+    left, right = seam_call(cov, tail, lax.axis_size("col"))
+    blended = blend(left, cov, right)
     return logits.reshape(1, 1, *logits.shape), blended
 
 

time: 25.3 us -> 25.4 us (level)
  other arithmetic: 0 us -> 1.98 us
  local copies, waits for them, and re-layouts: 1.38 us -> 0 us
  Pallas kernels: 23.1 us -> 22.6 us
    add x0 -> x1, other arithmetic: none -> 1.98 us  [blend(): blended = blended + factor * padded[:, SEAM + offset:SEAM + offset + side]]
    unnamed x1 -> x0, local copies, waits for them, and re-layouts: 1.38 us -> none
    pallas_call x1, Pallas kernels: 6.09 us -> 5.57 us  [seam_call(): pl.pallas_call(functools.partial(seam_kernel, n), out_shape=(jax.ShapeDty...]
where the time goes in v4:
time: 25.4 us; the launch traced here: 25.2 us
  Pallas kernels  22.6 us (89%)
  other arithmetic  1.98 us (8%)
  between operations  0.65 us (3%)
    pallas_call x1, Pallas kernels, tile_call(): pl.pallas_call(tile_kernel, out_shape=(jax.ShapeDtypeStruct((slots, cells...  17 us
    pallas_call x1, Pallas kernels, seam_call(): pl.pallas_call(functools.partial(seam_kernel, n), out_shape=(jax.ShapeDty...  5.57 us
    add x1, other arithmetic, blend(): blended = blended + factor * padded[:, SEAM + offset:SEAM + offset + side]  1.98 us

profile of v4, /device:TPU:97, one launch (start us, length us, event | category | flops | bytes accessed | tf_op | source)
XLA Modules:
  0.0 25.2 jit_solution(417101027804552322)
XLA Ops:
  0.6 17.0 %tile.1 = (bf16[48,4096]{1,0:T(8,128)(2,1)}, f32[64,64]{1,0:T(8,128)}, f32[64,64]{1,0:T(8,128)}) custom-call(s32[1,16]{1,0:T(1,128)} %counts_ref.1, s32[2,48]{1,0:T(2,128)} %bitcast.10, f32[2,128]{1,0:T(2,128)} %gauss_ref.1, f32[1,256]{1,0:T(1,128)} %bitcast.11, f32[1,256]{1,0:T(1,128)} %bitcast.12, f32[4,256]{1,0:T(4,128)} %gains_ref.1, ...), custom_call_target="tpu_custom_call" | custom-call | tf_op jit(solution)/shard_map/tile/pallas_call | solution.py:446
  17.6 5.6 %seam.1 = (f32[64,64]{1,0:T(8,128)}, f32[64,64]{1,0:T(8,128)}) custom-call(f32[64,64]{1,0:T(8,128)} %get-tuple-element.8.cov_hbm, f32[64,64]{1,0:T(8,128)} %get-tuple-element.9.tail_hbm), custom_call_target="tpu_custom_call" | custom-call | tf_op jit(solution)/shard_map/seam/pallas_call | solution.py:484
  23.2 2.0 %fusion.1 = f32[64,64]{1,0:T(8,128)} fusion(f32[64,4]{1,0:T(8,128)} %bitcast.9, f32[64,64]{1,0:T(8,128)} %get-tuple-element.8.cov_hbm, f32[64,4]{1,0:T(8,128)} %bitcast.8), kind=kLoop, calls=%fused_computation.2 | loop fusion | flops 102400 | bytes 34816 | tf_op jit(solution)/shard_map/add | solution.py:506

commit v5 on v4

--- a/solution.py
+++ b/solution.py
@@ -112,7 +112,6 @@
     hyper_hbm,
     logits_hbm,
     cov_ref,
-    tail_ref,
     emb_ref,
     sa_qkv_ref,
     sa_out_ref,
@@ -357,15 +356,13 @@
         out_copies.append(pltpu.make_async_copy(logits_ref.at[:, here], logits_hbm.at[:, here], out_sem.at[at // IMAGE_CELLS]))
         out_copies[-1].start()
         cover = jnp.sum(jnp.where(live, jax.nn.sigmoid(masked), 0.0), axis=0, keepdims=True)
-        for k0 in range(0, IMAGE_CELLS, side):
-            cov_ref[(at + k0) // side : (at + k0) // side + 1, :] = cover[:, k0 : k0 + side]
-    cov = cov_ref[...]
-    tail_ref[...] = jnp.concatenate([cov[:, side - SEAM :], cov[:, : side - SEAM]], axis=1)
+        for k0 in range(0, IMAGE_CELLS, LANES):
+            cov_ref[(at + k0) // LANES : (at + k0) // LANES + 1, :] = cover[:, k0 : k0 + LANES]
     for copy in out_copies:
         copy.wait()
 
 
-def seam_kernel(n, cov_hbm, tail_hbm, left_hbm, right_hbm, zero_ref, send_sem, recv_sem, zero_sem):
+def seam_kernel(n, cov_hbm, left_hbm, right_hbm, zero_ref, send_sem, recv_sem, zero_sem):
     me = lax.axis_index("col")
     has_left, has_right = me > 0, me < n - 1
     barrier = pltpu.get_barrier_semaphore()
@@ -383,7 +380,7 @@
 
     def to_right():
         return pltpu.make_async_remote_copy(
-            src_ref=tail_hbm,
+            src_ref=cov_hbm,
             dst_ref=left_hbm,
             send_sem=send_sem.at[1],
             recv_sem=recv_sem.at[1],
@@ -447,11 +444,10 @@
         tile_kernel,
         out_shape=(
             jax.ShapeDtypeStruct((slots, cells), BF16),
-            jax.ShapeDtypeStruct((math.isqrt(cells),) * 2, F32),
-            jax.ShapeDtypeStruct((math.isqrt(cells),) * 2, F32),
+            jax.ShapeDtypeStruct((cells // LANES, LANES), F32),
         ),
         in_specs=[pl.BlockSpec(memory_space=pltpu.SMEM)] + [vmem] * 5 + [hbm] * len(large),
-        out_specs=(hbm, vmem, vmem),
+        out_specs=(hbm, vmem),
         scratch_shapes=[pltpu.VMEM(a.shape, a.dtype) for a in large]
         + [
             pltpu.VMEM((slots, cells), BF16),
@@ -479,12 +475,12 @@
     )(counts, points, gauss, prompt, mask, gains, *large)
 
 
-def seam_call(cov, tail, n):
+def seam_call(cov, n):
     hbm = pl.BlockSpec(memory_space=pl.ANY)
     return pl.pallas_call(
         functools.partial(seam_kernel, n),
         out_shape=(jax.ShapeDtypeStruct(cov.shape, F32), jax.ShapeDtypeStruct(cov.shape, F32)),
-        in_specs=[hbm, hbm],
+        in_specs=[hbm],
         out_specs=(hbm, hbm),
         scratch_shapes=[
             pltpu.VMEM(cov.shape, F32),
@@ -494,17 +490,32 @@
         ],
         compiler_params=pltpu.CompilerParams(collective_id=0, has_side_effects=True),
         name="seam",
-    )(cov, tail)
-
-
-def blend(left, cov, right):
-    side = cov.shape[1]
-    padded = jnp.concatenate([left[:, :SEAM], cov, right[:, :SEAM]], axis=1)
-    blended = jnp.zeros_like(cov)
-    for offset in range(-SEAM, SEAM + 1):
-        factor = (SEAM + 1 - abs(offset)) / (SEAM + 1) ** 2
-        blended = blended + factor * padded[:, SEAM + offset : SEAM + offset + side]
-    return blended
+    )(cov)
+
+
+def blend_kernel(left_ref, cov_ref, right_ref, out_ref):
+    side = out_ref.shape[0]
+    left, cov, right = left_ref[...], cov_ref[...], right_ref[...]
+    x = lax.broadcasted_iota(jnp.int32, cov.shape, 1) % side
+    total = (SEAM + 1.0) * cov
+    for d in range(1, SEAM + 1):
+        after = jnp.where(x < side - d, pltpu.roll(cov, LANES - d, 1), pltpu.roll(right, side - d, 1))
+        before = jnp.where(x >= d, pltpu.roll(cov, d, 1), pltpu.roll(left, side + d, 1))
+        total = total + (SEAM + 1.0 - d) * (after + before)
+    total = total * (1.0 / (SEAM + 1) ** 2)
+    out_ref[pl.ds(0, side // 2, stride=2), :] = total[:, :side]
+    out_ref[pl.ds(1, side // 2, stride=2), :] = total[:, side:]
+
+
+def blend(left, cov, right, side):
+    vmem = pl.BlockSpec(memory_space=pltpu.VMEM)
+    return pl.pallas_call(
+        blend_kernel,
+        out_shape=jax.ShapeDtypeStruct((side, side), F32),
+        in_specs=[vmem] * 3,
+        out_specs=vmem,
+        name="blend",
+    )(left, cov, right)
 
 
 def shards(
@@ -526,7 +537,7 @@
     ln_gains,
 ):
     side, _, width = embedding.shape
-    logits, cov, tail = tile_call(
+    logits, cov = tile_call(
         counts,
         embedding.reshape(side * side, width),
         points[0, 0],
@@ -544,8 +555,8 @@
         hyper_w,
         ln_gains,
     )
-    left, right = seam_call(cov, tail, lax.axis_size("col"))
-    blended = blend(left, cov, right)
+    left, right = seam_call(cov, lax.axis_size("col"))
+    blended = blend(left, cov, right, side)
     return logits.reshape(1, 1, *logits.shape), blended
 
 

time: 25.4 us -> 24.8 us (0.976)
  other arithmetic: 1.98 us -> 0 us
  Pallas kernels: 22.6 us -> 23.9 us
    add x1 -> x0, other arithmetic: 1.98 us -> none  [blend(): blended = blended + factor * padded[:, SEAM + offset:SEAM + offset + side]]
    pallas_call x0 -> x1, Pallas kernels: none -> 1.57 us  [blend(): pl.pallas_call(blend_kernel, out_shape=jax.ShapeDtypeStruct((side, side),...]
where the time goes in v5:
time: 24.8 us; the launch traced here: 24.6 us
  Pallas kernels  23.9 us (96%)
  between operations  0.65 us (3%)
    pallas_call x1, Pallas kernels, tile_call(): pl.pallas_call(tile_kernel, out_shape=(jax.ShapeDtypeStruct((slots, cells...  17 us
    pallas_call x1, Pallas kernels, seam_call(): pl.pallas_call(functools.partial(seam_kernel, n), out_shape=(jax.ShapeDty...  5.38 us
    pallas_call x1, Pallas kernels, blend(): pl.pallas_call(blend_kernel, out_shape=jax.ShapeDtypeStruct((side, side),...  1.57 us

profile of v5, /device:TPU:97, one launch (start us, length us, event | category | flops | bytes accessed | tf_op | source)
XLA Modules:
  0.0 24.6 jit_solution(1232482085511922645)
XLA Ops:
  0.6 17.0 %tile.1 = (bf16[48,4096]{1,0:T(8,128)(2,1)}, f32[32,128]{1,0:T(8,128)}) custom-call(s32[1,16]{1,0:T(1,128)} %counts_ref.1, s32[2,48]{1,0:T(2,128)} %bitcast.6, f32[2,128]{1,0:T(2,128)} %gauss_ref.1, f32[1,256]{1,0:T(1,128)} %bitcast.7, f32[1,256]{1,0:T(1,128)} %bitcast.8, f32[4,256]{1,0:T(4,128)} %gains_ref.1, bf16[4096,256]{1,0:T(8,128)(2,1)} %bitcast.5, ...), custom_call_target="tpu_custom_call" | custom-call | tf_op jit(solution)/shard_map/tile/pallas_call | solution.py:443
  17.6 5.4 %seam.1 = (f32[32,128]{1,0:T(8,128)}, f32[32,128]{1,0:T(8,128)}) custom-call(f32[32,128]{1,0:T(8,128)} %get-tuple-element.7.cov_hbm.cov_ref), custom_call_target="tpu_custom_call" | custom-call | tf_op jit(solution)/shard_map/seam/pallas_call | solution.py:480
  23.0 1.6 %blend.1 = f32[64,64]{1,0:T(8,128)} custom-call(f32[32,128]{1,0:T(8,128)} %get-tuple-element.8.left_ref, f32[32,128]{1,0:T(8,128)} %get-tuple-element.7.cov_hbm.cov_ref, f32[32,128]{1,0:T(8,128)} %get-tuple-element.9.right_ref), custom_call_target="tpu_custom_call" | custom-call | tf_op jit(solution)/shard_map/blend/pallas_call | solution.py:512

commit v6 on v5

--- a/solution.py
+++ b/solution.py
@@ -111,7 +111,7 @@
     i2t_out_hbm,
     hyper_hbm,
     logits_hbm,
-    cov_ref,
+    cov_hbm,
     emb_ref,
     sa_qkv_ref,
     sa_out_ref,
@@ -141,6 +141,8 @@
     in_sem,
     emb_sem,
     out_sem,
+    cov_ref,
+    cov_sem,
 ):
     cells, width = emb_ref.shape
     slots = points_ref.shape[1]
@@ -358,6 +360,8 @@
         cover = jnp.sum(jnp.where(live, jax.nn.sigmoid(masked), 0.0), axis=0, keepdims=True)
         for k0 in range(0, IMAGE_CELLS, LANES):
             cov_ref[(at + k0) // LANES : (at + k0) // LANES + 1, :] = cover[:, k0 : k0 + LANES]
+    out_copies.append(pltpu.make_async_copy(cov_ref, cov_hbm, cov_sem))
+    out_copies[-1].start()
     for copy in out_copies:
         copy.wait()
 
@@ -447,7 +451,7 @@
             jax.ShapeDtypeStruct((cells // LANES, LANES), F32),
         ),
         in_specs=[pl.BlockSpec(memory_space=pltpu.SMEM)] + [vmem] * 5 + [hbm] * len(large),
-        out_specs=(hbm, vmem),
+        out_specs=(hbm, hbm),
         scratch_shapes=[pltpu.VMEM(a.shape, a.dtype) for a in large]
         + [
             pltpu.VMEM((slots, cells), BF16),
@@ -469,6 +473,8 @@
             pltpu.SemaphoreType.DMA((len(large) - 1,)),
             pltpu.SemaphoreType.DMA((EMB_COPIES,)),
             pltpu.SemaphoreType.DMA((cells // IMAGE_CELLS,)),
+            pltpu.VMEM((cells // LANES, LANES), F32),
+            pltpu.SemaphoreType.DMA(()),
         ],
         compiler_params=pltpu.CompilerParams(vmem_limit_bytes=58 * 2**20),
         name="tile",

time: 24.8 us -> 24.2 us (0.976)
  Pallas kernels: 23.9 us -> 23.3 us
    pallas_call x1, Pallas kernels: 17 us -> 16.4 us  [tile_call(): pl.pallas_call(tile_kernel, out_shape=(jax.ShapeDtypeStruct((slots, cells...]
where the time goes in v6:
time: 24.2 us; the launch traced here: 24 us
  Pallas kernels  23.3 us (96%)
  between operations  0.65 us (3%)
    pallas_call x1, Pallas kernels, tile_call(): pl.pallas_call(tile_kernel, out_shape=(jax.ShapeDtypeStruct((slots, cells...  16.4 us
    pallas_call x1, Pallas kernels, seam_call(): pl.pallas_call(functools.partial(seam_kernel, n), out_shape=(jax.ShapeDty...  5.38 us
    pallas_call x1, Pallas kernels, blend(): pl.pallas_call(blend_kernel, out_shape=jax.ShapeDtypeStruct((side, side),...  1.57 us

profile of v6, /device:TPU:97, one launch (start us, length us, event | category | flops | bytes accessed | tf_op | source)
XLA Modules:
  0.0 24.0 jit_solution(17268172689038029186)
XLA Ops:
  0.6 16.4 %tile.1 = (bf16[48,4096]{1,0:T(8,128)(2,1)}, f32[32,128]{1,0:T(8,128)}) custom-call(s32[1,16]{1,0:T(1,128)} %counts_ref.1, s32[2,48]{1,0:T(2,128)} %bitcast.6, f32[2,128]{1,0:T(2,128)} %gauss_ref.1, f32[1,256]{1,0:T(1,128)} %bitcast.7, f32[1,256]{1,0:T(1,128)} %bitcast.8, f32[4,256]{1,0:T(4,128)} %gains_ref.1, bf16[4096,256]{1,0:T(8,128)(2,1)} %bitcast.5, ...), custom_call_target="tpu_custom_call" | custom-call | tf_op jit(solution)/shard_map/tile/pallas_call | solution.py:447
  17.0 5.4 %seam.1 = (f32[32,128]{1,0:T(8,128)}, f32[32,128]{1,0:T(8,128)}) custom-call(f32[32,128]{1,0:T(8,128)} %get-tuple-element.7.cov_hbm.cov_ref), custom_call_target="tpu_custom_call" | custom-call | tf_op jit(solution)/shard_map/seam/pallas_call | solution.py:486
  22.4 1.6 %blend.1 = f32[64,64]{1,0:T(8,128)} custom-call(f32[32,128]{1,0:T(8,128)} %get-tuple-element.8.left_ref, f32[32,128]{1,0:T(8,128)} %get-tuple-element.7.cov_hbm.cov_ref, f32[32,128]{1,0:T(8,128)} %get-tuple-element.9.right_ref), custom_call_target="tpu_custom_call" | custom-call | tf_op jit(solution)/shard_map/blend/pallas_call | solution.py:518

commit v7 on v6

--- a/solution.py
+++ b/solution.py
@@ -332,11 +332,18 @@
     t_ref[:, heads:, :] = jnp.ones((GROUPS, blank, cells), BF16)
 
     out_copies = []
-    for at in range(0, cells, IMAGE_CELLS):
+
+    def two_token(at):
         here = slice(at, at + IMAGE_CELLS)
         t = jnp.tanh(dot_t(gap_ref[...], keys_ref[here, :])).astype(BF16)
         for n in range(GROUPS):
             t_ref[n, :heads, here] = t[n * heads : (n + 1) * heads]
+
+    two_token(0)
+    for at in range(0, cells, IMAGE_CELLS):
+        here = slice(at, at + IMAGE_CELLS)
+        if at + IMAGE_CELLS < cells:
+            two_token(at + IMAGE_CELLS)
         cell_part = dot_t(row_ref[...], emb_ref[here, :])
         sums = cell_part[GROUPS * lines : GROUPS * lines + 8]
         e = emb_ref[here, :].astype(F32)
@@ -345,7 +352,7 @@
         logits = []
         for n in range(GROUPS):
             line = cell_part[n * lines : (n + 1) * lines] + dot(mix_ref[n], t_ref[n, :, here])
-            t32 = t[n * heads : (n + 1) * heads].astype(F32)
+            t32 = t_ref[n, :heads, here].astype(F32)
             var = line[heads : heads + group] + jnp.concatenate([own] * (group // 8), axis=0)
             for h in range(HEADS):
                 var = var + t32[h * group : (h + 1) * group] * line[h * group : (h + 1) * group]

time: 24.2 us -> 24.2 us (level)
  no operation moved by 1% of the time
where the time goes in v7:
time: 24.2 us; the launch traced here: 24.1 us
  Pallas kernels  23.4 us (97%)
  between operations  0.65 us (3%)
    pallas_call x1, Pallas kernels, tile_call(): pl.pallas_call(tile_kernel, out_shape=(jax.ShapeDtypeStruct((slots, cells...  16.4 us
    pallas_call x1, Pallas kernels, seam_call(): pl.pallas_call(functools.partial(seam_kernel, n), out_shape=(jax.ShapeDty...  5.38 us
    pallas_call x1, Pallas kernels, blend(): pl.pallas_call(blend_kernel, out_shape=jax.ShapeDtypeStruct((side, side),...  1.57 us

profile of v7, /device:TPU:97, one launch (start us, length us, event | category | flops | bytes accessed | tf_op | source)
XLA Modules:
  0.0 24.1 jit_solution(10488238620024856947)
XLA Ops:
  0.6 16.4 %tile.1 = (bf16[48,4096]{1,0:T(8,128)(2,1)}, f32[32,128]{1,0:T(8,128)}) custom-call(s32[1,16]{1,0:T(1,128)} %counts_ref.1, s32[2,48]{1,0:T(2,128)} %bitcast.6, f32[2,128]{1,0:T(2,128)} %gauss_ref.1, f32[1,256]{1,0:T(1,128)} %bitcast.7, f32[1,256]{1,0:T(1,128)} %bitcast.8, f32[4,256]{1,0:T(4,128)} %gains_ref.1, bf16[4096,256]{1,0:T(8,128)(2,1)} %bitcast.5, ...), custom_call_target="tpu_custom_call" | custom-call | tf_op jit(solution)/shard_map/tile/pallas_call | solution.py:454
  17.1 5.4 %seam.1 = (f32[32,128]{1,0:T(8,128)}, f32[32,128]{1,0:T(8,128)}) custom-call(f32[32,128]{1,0:T(8,128)} %get-tuple-element.7.cov_hbm.cov_ref), custom_call_target="tpu_custom_call" | custom-call | tf_op jit(solution)/shard_map/seam/pallas_call | solution.py:493
  22.5 1.6 %blend.1 = f32[64,64]{1,0:T(8,128)} custom-call(f32[32,128]{1,0:T(8,128)} %get-tuple-element.8.left_ref, f32[32,128]{1,0:T(8,128)} %get-tuple-element.7.cov_hbm.cov_ref, f32[32,128]{1,0:T(8,128)} %get-tuple-element.9.right_ref), custom_call_target="tpu_custom_call" | custom-call | tf_op jit(solution)/shard_map/blend/pallas_call | solution.py:525
